TPU v7x, 32 devices: a whole 2x2x4 slice. The times are simulated.
32 devices in a mesh: prompt: 8 (over z, core), resp: 4 (over y, x).
Axes of the slice: x: 2, y: 2, z: 4, core: 2. Of those that a mesh axis runs over, the one named last changes fastest.
Arguments:
- inputs: bfloat16 [32, 128, 16384], P(('prompt', 'resp')), parts along dimension 0, may hold values from -6 to 6
- cotangent: bfloat16 [32, 128, 16384], P(('prompt', 'resp')), parts along dimension 0, may hold values from -96 to 96
- b_proj: bfloat16 [32, 128, 2048], P(('prompt', 'resp')), parts along dimension 0, may hold values from -0.375 to 0.375
- c_proj: bfloat16 [32, 128, 2048], P(('prompt', 'resp')), parts along dimension 0, may hold values from -0.375 to 0.375
- dt_raw: float32 [32, 128, 256], P(('prompt', 'resp')), parts along dimension 0, may hold values from -6 to 6
- decay_rate: float32 [256], replicated, may hold values from 0.003 to 0.06
- state_codes: bfloat16 [2048, 64, 256], P(('prompt', 'resp')), parts along dimension 0, may hold values from -6 to 6
- state_scales: bfloat16 [2048, 64], P(('prompt', 'resp')), parts along dimension 0, may hold values from 0.25 to 2
- sign_bucket: int32 [32], P(('prompt', 'resp')), parts along dimension 0, may hold values from 0 to 1
- adv_scale: float32 [32], P(('prompt', 'resp')), parts along dimension 0, may hold values from 0.5 to 2
- lengths: int32 [32], P(('prompt', 'resp')), parts along dimension 0, may hold values from 64 to 128, as said below
Outputs:
- grad_state: float32 [2048, 64, 256], P(('prompt', 'resp')), parts along dimension 0
- grad_b: bfloat16 [32, 128, 2048], P(('prompt', 'resp')), parts along dimension 0
- grad_c: bfloat16 [32, 128, 2048], P(('prompt', 'resp')), parts along dimension 0
- grad_dt: float32 [32, 128, 256], P(('prompt', 'resp')), parts along dimension 0
There are 8 independent parts, one for each index of `prompt`. A program takes and returns all parts, laid end to end along the dimension named above; an argument that names none is the same for every part. Nothing has to cross between parts.
Inputs may be any that keep to these rules, and one draw needn't show every extreme that they name: `lengths`: every response has at least 64 valid tokens; some response of each prompt has exactly 128.
All inputs are finite; a program needn't handle non-finite values.
Results may differ from a plain program's by a relative error of at most 0.001.
Values may be sent and summed in bfloat16 or wider, within the bound.
A program may use at most 128 MiB of HBM per device.

v0:
```python
import jax
import jax.numpy as jnp
from jax import lax
from jax.sharding import PartitionSpec as P


def group_forward(group_x, scores, group_c, group_dt, group_rate, group_state):
    tok_rows = group_x.shape[0]
    head_count = group_dt.shape[1]
    step_size = jax.nn.softplus(group_dt)
    log_decay = jnp.cumsum(-step_size * group_rate[None, :], axis=0)
    decay_rows = log_decay.T
    decay_gap = decay_rows[:, :, None] - decay_rows[:, None, :]
    causal = (
        jnp.arange(tok_rows, dtype=jnp.int32)[:, None]
        >= jnp.arange(tok_rows, dtype=jnp.int32)[None, :]
    )
    attenuation = jnp.where(causal[None], jnp.exp(jnp.where(causal[None], decay_gap, 0.0)), 0.0)
    mixing = attenuation * scores[None] * step_size.T[:, None, :]
    head_x = group_x.reshape(tok_rows, head_count, -1)
    within = jnp.einsum("hts,shp->thp", mixing, head_x, precision=lax.Precision.HIGHEST)
    carried = jnp.exp(log_decay)[:, :, None] * jnp.einsum(
        "tn,hpn->thp", group_c, group_state, precision=lax.Precision.HIGHEST
    )
    return (within + carried).reshape(tok_rows, -1)


def response_grads(x_rows, up_rows, b_rows, c_rows, dt_rows, rate, prefix_state, row_coef):
    state_dim = prefix_state.shape[2]
    head_dim = prefix_state.shape[1]
    group_count = b_rows.shape[1] // state_dim
    group_heads = rate.shape[0] // group_count
    group_width = group_heads * head_dim
    tok_rows = x_rows.shape[0]

    def one_group(group_idx):
        group_x = lax.dynamic_slice_in_dim(x_rows, group_idx * group_width, group_width, 1).astype(
            jnp.float32
        )
        group_dy = (
            lax.dynamic_slice_in_dim(up_rows, group_idx * group_width, group_width, 1).astype(
                jnp.float32
            )
            * row_coef[:, None]
        )
        b_half = lax.dynamic_slice_in_dim(b_rows, group_idx * state_dim, state_dim, 1)
        c_half = lax.dynamic_slice_in_dim(c_rows, group_idx * state_dim, state_dim, 1)
        group_b = b_half.astype(jnp.float32)
        group_c = c_half.astype(jnp.float32)
        scores = jnp.dot(c_half, b_half.T, preferred_element_type=jnp.float32)
        group_dt = lax.dynamic_slice_in_dim(dt_rows, group_idx * group_heads, group_heads, 1)
        group_rate = lax.dynamic_slice_in_dim(rate, group_idx * group_heads, group_heads, 0)
        group_state = lax.dynamic_slice_in_dim(
            prefix_state, group_idx * group_heads, group_heads, 0
        )

        def forward(s_in, c_in, dt_in, state_in):
            return group_forward(group_x, s_in, c_in, dt_in, group_rate, state_in)

        result, pullback = jax.vjp(forward, scores, group_c, group_dt, group_state)
        grads = pullback(group_dy)
        d_scores = grads[0]
        grad_b = jnp.dot(d_scores.T, group_c, precision=lax.Precision.HIGHEST)
        grad_c = jnp.dot(d_scores, group_b, precision=lax.Precision.HIGHEST) + grads[1]
        return (grad_b, grad_c) + tuple(grads[2:])

    results = lax.map(one_group, jnp.arange(group_count, dtype=jnp.int32))
    grad_b = results[0].transpose(1, 0, 2).reshape(tok_rows, -1)
    grad_c = results[1].transpose(1, 0, 2).reshape(tok_rows, -1)
    grad_dt = results[2].transpose(1, 0, 2).reshape(tok_rows, -1)
    return (grad_b, grad_c, grad_dt, results[3].reshape(rate.shape[0], head_dim, state_dim))


def per_device(
    inputs,
    cotangent,
    b_proj,
    c_proj,
    dt_raw,
    decay_rate,
    state_codes,
    state_scales,
    sign_bucket,
    adv_scale,
    lengths,
):
    codes_all, scales_all = (
        lax.all_gather(state_codes, "resp", axis=0, tiled=True),
        lax.all_gather(state_scales, "resp", axis=0, tiled=True),
    )
    prefix_state = codes_all.astype(jnp.float32) * scales_all.astype(jnp.float32)[:, :, None]
    tok_rows = inputs.shape[1]
    sign_value = 2.0 * sign_bucket[0].astype(jnp.float32) - 1.0
    coefficient = sign_value * adv_scale[0] / lengths[0].astype(jnp.float32)
    row_coef = jnp.where(
        jnp.arange(tok_rows, dtype=jnp.int32) < lengths[0], coefficient, jnp.zeros((), jnp.float32)
    )
    grad_b, grad_c, grad_dt, grad_part = response_grads(
        inputs[0], cotangent[0], b_proj[0], c_proj[0], dt_raw[0], decay_rate, prefix_state, row_coef
    )
    grad_state = lax.psum_scatter(grad_part, "resp", scatter_dimension=0, tiled=True)
    return (
        grad_state,
        grad_b.astype(jnp.bfloat16)[None],
        grad_c.astype(jnp.bfloat16)[None],
        grad_dt[None],
    )


def solution(mesh):
    return jax.shard_map(
        per_device,
        mesh=mesh,
        in_specs=(
            P(("prompt", "resp"), None, None),
            P(("prompt", "resp"), None, None),
            P(("prompt", "resp"), None, None),
            P(("prompt", "resp"), None, None),
            P(("prompt", "resp"), None, None),
            P(),
            P(("prompt", "resp"), None, None),
            P(("prompt", "resp"), None),
            P(("prompt", "resp")),
            P(("prompt", "resp")),
            P(("prompt", "resp")),
        ),
        out_specs=(
            P(("prompt", "resp"), None, None),
            P(("prompt", "resp"), None, None),
            P(("prompt", "resp"), None, None),
            P(("prompt", "resp"), None, None),
        ),
        check_vma=False,
    )
```

profile of v0, /device:TPU:0, one launch (start us, length us, event | category | flops | bytes accessed | tf_op | source)
XLA Modules:
  0.0 446.2 jit_solution(8823699201582352811)
XLA Ops:
  9.9 9.8 %all_gather.7 = bf16[256,64]{1,0:T(8,128)(2,1)S(1)} all-gather(bf16[64,64]{1,0:T(8,128)(2,1)} %param.20), channel_id=1, replica_groups=mesh['prompt'=8,'resp'=4] {'resp'}, dimensions={0}, use_global_device_ids=true | all-gather | bytes 40960 | tf_op jit(solution)/shard_map/all_gather | solution.py:89
  19.8 6.6 %copy.55 = bf16[1,128,16384]{1,2,0:T(8,128)(2,1)} copy(bf16[1,128,16384]{2,1,0:T(8,128)(2,1)} %param.13) | data formatting | bytes 8388608 | tf_op args[0]
  26.4 6.4 %copy.54 = bf16[1,128,16384]{1,2,0:T(8,128)(2,1)} copy(bf16[1,128,16384]{2,1,0:T(8,128)(2,1)} %param.14) | data formatting | bytes 8388608 | tf_op args[1]
  32.9 67.3 %all-gather.2.cloned.1.call-done = bf16[256,64,256]{2,1,0:T(8,128)(2,1)} async-done(((bf16[64,64,256]{2,1,0:T(8,128)(2,1)}), bf16[256,64,256]{2,1,0:T(8,128)(2,1)}) %all-gather.2.cloned.1.call-update) | async-done | bytes 8388624 | tf_op jit(solution)/shard_map/all_gather | solution.py:88
  100.2 10.2 %convert_multiply_fusion.1 = f32[256,64,256]{2,1,0:T(8,128)} fusion(bf16[256,64,256]{2,1,0:T(8,128)(2,1)} %all-gather.2.cloned.1.call-done, f32[256,64]{1,0:T(8,128)S(1)} %convert_element_type.54), kind=kLoop, calls=%fused_computation.56 | loop fusion | flops 8388608 | bytes 25231360 | tf_op jit(solution)/shard_map/mul | solution.py:91
  110.4 174.9 %while.17 = (s32[]{:T(128)}, bf16[8,128,256]{2,1,0:T(8,128)(2,1)S(1)}, bf16[8,128,256]{2,1,0:T(8,128)(2,1)S(1)}, f32[8,128,32]{1,2,0:T(8,128)S(1)}, f32[8,32,64,...) while((s32[]{:T(128)}, ...), condition=%wide.region_8.9_spmd.clone, body=%wide.region_0.8_spmd.clone.sunk | while | flops 2938228992 | bytes 15551423 | solution.py:67
  115.2 1.1 constant_dynamic-slice_fusion.2
  116.3 1.1 convert_multiply_fusion.3
  117.4 3.5 fusion.85
  120.9 2.7 fusion.87
  123.7 1.1 reduce_window_sum.27
  125.1 3.5 fusion.88
  128.6 1.1 fusion.89
  129.9 2.3 bitcast_dynamic-update-slice_fusion.2
  137.1 1.1 constant_dynamic-slice_fusion.2
  138.2 1.1 convert_multiply_fusion.3
  139.3 3.5 fusion.85
  142.8 2.7 fusion.87
  145.5 1.1 reduce_window_sum.27
  147.0 3.5 fusion.88
  151.8 2.3 bitcast_dynamic-update-slice_fusion.2
  158.9 1.1 constant_dynamic-slice_fusion.2
  160.0 1.1 convert_multiply_fusion.3
  161.1 3.5 fusion.85
  164.6 2.7 fusion.87
  167.4 1.1 reduce_window_sum.27
  168.8 3.5 fusion.88
  173.6 2.3 bitcast_dynamic-update-slice_fusion.2
  180.7 1.1 constant_dynamic-slice_fusion.2
  181.9 1.1 convert_multiply_fusion.3
  183.0 3.5 fusion.85
  186.5 2.7 fusion.87
  189.2 1.1 reduce_window_sum.27
  190.7 3.5 fusion.88
  195.5 2.3 bitcast_dynamic-update-slice_fusion.2
  202.6 1.1 constant_dynamic-slice_fusion.2
  203.7 1.1 convert_multiply_fusion.3
  204.8 3.5 fusion.85
  208.3 2.7 fusion.87
  211.1 1.1 reduce_window_sum.27
  212.5 3.5 fusion.88
  217.4 2.4 bitcast_dynamic-update-slice_fusion.2
  224.5 1.1 constant_dynamic-slice_fusion.2
  225.6 1.1 convert_multiply_fusion.3
  226.8 3.5 fusion.85
  230.3 2.7 fusion.87
  233.0 1.1 reduce_window_sum.27
  234.5 3.5 fusion.88
  239.3 2.3 bitcast_dynamic-update-slice_fusion.2
  246.4 1.1 constant_dynamic-slice_fusion.2
  247.5 1.1 convert_multiply_fusion.3
  248.6 3.5 fusion.85
  252.1 2.7 fusion.87
  254.9 1.1 reduce_window_sum.27
  256.3 3.5 fusion.88
  261.1 2.3 bitcast_dynamic-update-slice_fusion.2
  268.3 1.1 constant_dynamic-slice_fusion.2
  269.4 1.1 convert_multiply_fusion.3
  270.5 3.5 fusion.85
  274.0 2.7 fusion.87
  276.7 1.1 reduce_window_sum.27
  278.2 3.5 fusion.88
  283.0 2.3 bitcast_dynamic-update-slice_fusion.2
  288.7 150.6 %reduce-scatter.2.cloned.1.call-done = f32[64,64,256]{2,1,0:T(8,128)} async-done(((f32[256,64,256]{2,1,0:T(8,128)}), f32[64,64,256]{2,1,0:T(8,128)}) %reduce-scatter.2.cloned.1.call-update) | async-done | bytes 4194320 | tf_op jit(solution)/shard_map/reduce_scatter | solution.py:101
  (164 shorter events, 39.5 us)
Async XLA Ops:
  7.2 93.0 %all-gather.2.cloned.1.call-start = ((), (), s32[]{:S(2)}) async-start(), calls=%async_computation.1 | async-start | bytes 10485760 | tf_op jit(solution)/shard_map/all_gather | solution.py:88
  7.9 431.4 %reduce-scatter.2.cloned.1.call-start = ((), (), s32[]{:S(2)}) async-start(), calls=%async_computation.2 | async-start | bytes 20971520 | tf_op jit(solution)/shard_map/reduce_scatter | solution.py:101
  32.8 77.5 %copy-start = (bf16[1,128,2048]{2,1,0:T(8,128)(2,1)S(1)}, bf16[1,128,2048]{2,1,0:T(8,128)(2,1)}, u32[]{:S(2)}) copy-start(bf16[1,128,2048]{2,1,0:T(8,128)(2,1)} %param.16) | copy-start | bytes 1572868
  32.8 77.5 %copy-start.1 = (f32[1,128,256]{2,1,0:T(8,128)S(1)}, f32[1,128,256]{2,1,0:T(8,128)}, u32[]{:S(2)}) copy-start(f32[1,128,256]{2,1,0:T(8,128)} %param.17) | copy-start | bytes 393220
  32.8 77.5 %copy-start.2 = (f32[256]{0:T(256)S(1)}, f32[256]{0:T(256)}, u32[]{:S(2)}) copy-start(f32[256]{0:T(256)} %param.18) | copy-start | bytes 3076
Sparse Core Ops, SparseCore 0:
  9.8 90.2 all-gather.1
  285.4 153.8 reduce-scatter.1
where the time goes:
time: 449 us; the launch traced here: 446 us
  waiting for transfers between devices  219 us (49%)
  matrix products  114 us (25%)
  other arithmetic  37.3 us (8%)
  local copies, waits for them, and re-layouts  34 us (8%)
  loops' own time  16.3 us (4%)
  between operations  16.1 us (4%)
  blocking collectives  9.85 us (2%)
    reduce_scatter x1, waiting for transfers between devices, per_device(): lax.psum_scatter(grad_part, 'resp', scatter_dimension=0, tiled=True)  151 us
    dot_general x24, matrix products, group_forward(): jnp.einsum('tn,hpn->thp', group_c, group_state, precision=lax.Precision.H...  67.7 us
    all_gather x1, waiting for transfers between devices, per_device(): lax.all_gather(state_codes, 'resp', axis=0, tiled=True)  67.3 us
    dot_general x8, matrix products, group_forward(): jnp.einsum('hts,shp->thp', mixing, head_x, precision=lax.Precision.HIGHEST)  27.8 us
    another operation x1, loops' own time, response_grads(): results = lax.map(one_group, jnp.arange(group_count, dtype=jnp.int32))  16.3 us
    unnamed x9, local copies, waits for them, and re-layouts  13.8 us
    another operation x16, other arithmetic, group_forward(): log_decay = jnp.cumsum(-step_size * group_rate[None, :], axis=0)  10.4 us
    mul x1, other arithmetic, per_device(): codes_all.astype(jnp.float32) * scales_all.astype(jnp.float32)[:, :, None]  10.2 us
  transfers between devices with their start and end apart: 2, of which 2 were waited for; matrix products, arithmetic and copies ran while one was open for 4% of the time, Pallas kernels for 0%

commit v1 on v0

v1 whole, which is shorter than its diff:
```python
import functools
import jax
import jax.numpy as jnp
from jax import lax
from jax.experimental import pallas as pl
from jax.experimental.pallas import tpu as pltpu
from jax.sharding import PartitionSpec as P

F32 = jnp.float32
BF16 = jnp.bfloat16
CHUNK = 512
VMEM_BYTES = 48 * 1024 * 1024


def dot(left, right):
    return lax.dot_general(left, right, (((1,), (0,)), ((), ())), preferred_element_type=F32)


def dot_nt(left, right):
    return lax.dot_general(left, right, (((1,), (1,)), ((), ())), preferred_element_type=F32)


def dot_tn(left, right):
    return lax.dot_general(left, right, (((0,), (0,)), ((), ())), preferred_element_type=F32)


def split(value):
    high = value.astype(BF16)
    return high, (value - high.astype(F32)).astype(BF16)


def three_parts(value):
    high = value.astype(BF16)
    rest = value - high.astype(F32)
    middle, low = split(rest)
    return jnp.concatenate([high, middle, low], axis=1)


def head_spread(heads, head_dim, start, width):
    row = lax.broadcasted_iota(jnp.int32, (heads, width), 0)
    col = lax.broadcasted_iota(jnp.int32, (heads, width), 1) + start
    first = row * head_dim
    one = jnp.where((col >= first) & (col < first + head_dim), 1.0, 0.0).astype(BF16)
    return jnp.concatenate([one, one, one], axis=0)


def head_gather(heads, head_dim, start, width):
    row = lax.broadcasted_iota(jnp.int32, (width, heads), 0) + start
    first = lax.broadcasted_iota(jnp.int32, (width, heads), 1) * head_dim
    return jnp.where((row >= first) & (row < first + head_dim), 1.0, 0.0).astype(BF16)


def within_kernel(
    head_dim, x_ref, d_ref, b_ref, c_ref, wa_ref, wb_ref, gb_ref, gc_ref, row_ref, col_ref, spread, gather
):
    heads = wa_ref.shape[2]
    tok, width = x_ref.shape
    chunk = min(CHUNK, width)

    @pl.when(pl.program_id(0) == 0)
    def _():
        spread[...] = head_spread(heads, head_dim, 0, width)
        gather[...] = head_gather(heads, head_dim, 0, width)

    b = b_ref[...]
    c = c_ref[...]
    at = lax.broadcasted_iota(jnp.int32, (tok, tok), 0)
    of = lax.broadcasted_iota(jnp.int32, (tok, tok), 1)
    s_hi, s_lo = split(jnp.where(at >= of, dot_nt(c, b), 0.0))
    scores = jnp.concatenate([s_hi, s_lo, s_hi], axis=1)
    t_hi, t_lo = split(jnp.where(at <= of, dot_nt(b, c), 0.0))
    flipped = jnp.concatenate([t_hi, t_lo, t_hi], axis=1)
    wa = three_parts(wa_ref[0])
    wb = three_parts(wb_ref[0])
    d_scores = jnp.zeros((tok, tok), F32)
    sums = jnp.zeros((4 * tok, heads), F32)
    for start in range(0, width, chunk):
        here = slice(start, start + chunk)
        ex = spread[:, here]
        w = d_ref[:, here].astype(F32) * dot(wa, ex)
        x = x_ref[:, here].astype(F32) * dot(wb, ex)
        w_hi, w_lo = split(w)
        x_hi, x_lo = split(x)
        d_scores += dot_nt(
            jnp.concatenate([w_hi, w_hi, w_lo], axis=1), jnp.concatenate([x_hi, x_lo, x_hi], axis=1)
        )
        p = w * dot(scores, jnp.concatenate([x_hi, x_hi, x_lo], axis=0))
        q = x * dot(flipped, jnp.concatenate([w_hi, w_hi, w_lo], axis=0))
        sums += dot(jnp.concatenate(split(p) + split(q), axis=0), gather[here, :])
    row_ref[0] = sums[:tok] + sums[tok : 2 * tok]
    col_ref[0] = sums[2 * tok : 3 * tok] + sums[3 * tok :]
    d_scores = jnp.where(at >= of, d_scores, 0.0)
    gc_ref[...] = dot(jnp.concatenate(split(d_scores), axis=1), jnp.concatenate([b, b], axis=0))
    gb_ref[...] = dot(
        jnp.concatenate(split(d_scores.T), axis=1), jnp.concatenate([c, c], axis=0)
    ).astype(BF16)


def within(x, d, b, c, wa, wb, head_dim):
    groups, tok, heads = wa.shape
    width = heads * head_dim
    state_dim = b.shape[1] // groups
    cols = lambda g: (0, g)
    lead = lambda g: (g, 0, 0)
    return pl.pallas_call(
        functools.partial(within_kernel, head_dim),
        grid=(groups,),
        in_specs=[
            pl.BlockSpec((tok, width), cols),
            pl.BlockSpec((tok, width), cols),
            pl.BlockSpec((tok, state_dim), cols),
            pl.BlockSpec((tok, state_dim), cols),
            pl.BlockSpec((1, tok, heads), lead),
            pl.BlockSpec((1, tok, heads), lead),
        ],
        out_specs=[
            pl.BlockSpec((tok, state_dim), cols),
            pl.BlockSpec((tok, state_dim), cols),
            pl.BlockSpec((1, tok, heads), lead),
            pl.BlockSpec((1, tok, heads), lead),
        ],
        out_shape=[
            jax.ShapeDtypeStruct(b.shape, BF16),
            jax.ShapeDtypeStruct(c.shape, F32),
            jax.ShapeDtypeStruct(wa.shape, F32),
            jax.ShapeDtypeStruct(wa.shape, F32),
        ],
        scratch_shapes=[pltpu.VMEM((3 * heads, width), BF16), pltpu.VMEM((width, heads), BF16)],
        compiler_params=pltpu.CompilerParams(vmem_limit_bytes=VMEM_BYTES),
        cost_estimate=pl.CostEstimate(
            flops=24 * tok * tok * x.shape[1], bytes_accessed=4 * x.size + 6 * b.size, transcendentals=0
        ),
        name="within",
    )(x, d, b, c, wa, wb)


def carried_kernel(head_dim, d_ref, c_ref, w_ref, codes_ref, scale_ref, dc_ref, dl_ref):
    heads = w_ref.shape[2]
    tok, width = d_ref.shape
    chunk = min(CHUNK, width)
    c = c_ref[...]
    wt = three_parts(w_ref[0])
    d_c = jnp.zeros((2 * tok, c.shape[1]), F32)
    sums = jnp.zeros((2 * tok, heads), F32)
    for start in range(0, width, chunk):
        here = slice(start, start + chunk)
        codes = codes_ref[here, :]
        w = d_ref[:, here].astype(F32) * dot(wt, head_spread(heads, head_dim, start, chunk))
        w = w * scale_ref[:, here]
        d_c += dot(jnp.concatenate(split(w), axis=0), codes)
        p = w * dot_nt(c, codes)
        sums += dot(jnp.concatenate(split(p), axis=0), head_gather(heads, head_dim, start, chunk))
    dc_ref[...] = d_c[:tok] + d_c[tok:]
    dl_ref[0] = sums[:tok] + sums[tok:]


def carried(d, c, w, codes, scale, head_dim):
    span, tok, heads = w.shape
    width = heads * head_dim
    state_dim = codes.shape[1]
    cols = lambda g: (0, g)
    return pl.pallas_call(
        functools.partial(carried_kernel, head_dim),
        grid=(span,),
        in_specs=[
            pl.BlockSpec((tok, width), cols),
            pl.BlockSpec((tok, state_dim), cols),
            pl.BlockSpec((1, tok, heads), lambda g: (g, 0, 0)),
            pl.BlockSpec((width, state_dim), lambda g: (g, 0)),
            pl.BlockSpec((1, width), cols),
        ],
        out_specs=[
            pl.BlockSpec((tok, state_dim), cols),
            pl.BlockSpec((1, tok, heads), lambda g: (g, 0, 0)),
        ],
        out_shape=[
            jax.ShapeDtypeStruct((tok, span * state_dim), F32),
            jax.ShapeDtypeStruct(w.shape, F32),
        ],
        compiler_params=pltpu.CompilerParams(vmem_limit_bytes=VMEM_BYTES),
        cost_estimate=pl.CostEstimate(
            flops=6 * tok * codes.size, bytes_accessed=2 * (d.size + codes.size), transcendentals=0
        ),
        name="carried",
    )(d, c, w, codes, scale)


def state_kernel(head_dim, count, *refs):
    out_ref = refs[-1]
    chunk, state_dim = out_ref.shape
    heads = refs[2 * count].shape[2]
    per_group = heads * head_dim // chunk
    start = lax.rem(pl.program_id(0), per_group) * chunk
    spread = head_spread(heads, head_dim, start, chunk)
    total = jnp.zeros((state_dim, chunk), F32)
    for i in range(count):
        d_ref, c_ref, w_ref = refs[i], refs[count + i], refs[2 * count + i]
        w = d_ref[...].astype(F32) * dot(three_parts(w_ref[0]), spread)
        c = c_ref[...]
        total += dot_tn(jnp.concatenate([c, c], axis=0), jnp.concatenate(split(w), axis=0))
    out_ref[...] = total.T


def state_gradient(ds, cs, ws, head_dim):
    span, tok, heads = ws[0].shape
    width = ds[0].shape[1]
    chunk = min(CHUNK, heads * head_dim)
    per_group = heads * head_dim // chunk
    state_dim = cs[0].shape[1] // span
    count = len(ds)
    return pl.pallas_call(
        functools.partial(state_kernel, head_dim, count),
        grid=(width // chunk,),
        in_specs=[pl.BlockSpec((tok, chunk), lambda j: (0, j))] * count
        + [pl.BlockSpec((tok, state_dim), lambda j: (0, j // per_group))] * count
        + [pl.BlockSpec((1, tok, heads), lambda j: (j // per_group, 0, 0))] * count,
        out_specs=pl.BlockSpec((chunk, state_dim), lambda j: (j, 0)),
        out_shape=jax.ShapeDtypeStruct((width, state_dim), F32),
        compiler_params=pltpu.CompilerParams(vmem_limit_bytes=VMEM_BYTES),
        cost_estimate=pl.CostEstimate(
            flops=4 * count * tok * width * state_dim,
            bytes_accessed=2 * count * tok * width + 4 * width * state_dim,
            transcendentals=0,
        ),
        name="state_gradient",
    )(*ds, *cs, *ws)


def per_device(
    count,
    inputs,
    cotangent,
    b_proj,
    c_proj,
    dt_raw,
    decay_rate,
    state_codes,
    state_scales,
    sign_bucket,
    adv_scale,
    lengths,
):
    x, d, b, c, dt = inputs[0], cotangent[0], b_proj[0], c_proj[0], dt_raw[0]
    tok, all_heads = dt.shape
    own, head_dim, state_dim = state_codes.shape
    groups = b.shape[1] // state_dim
    group_heads = all_heads // groups
    span = max(1, own // group_heads)
    part = own // span
    width = own * head_dim
    me = lax.axis_index("resp")

    step = jax.nn.softplus(dt)
    at = jnp.arange(tok, dtype=jnp.int32)
    lower = (at[:, None] >= at[None, :]).astype(F32)
    log_decay = -decay_rate[None, :] * jnp.dot(lower, step, precision=lax.Precision.HIGHEST)
    sign_value = 2.0 * sign_bucket[0].astype(F32) - 1.0
    coefficient = sign_value * adv_scale[0] / lengths[0].astype(F32)
    row_coef = jnp.where(at < lengths[0], coefficient, jnp.zeros((), F32))
    wa = row_coef[:, None] * jnp.exp(log_decay)
    wb = step * jnp.exp(-log_decay)

    def by_group(value, pieces):
        return value.reshape(tok, pieces, -1).transpose(1, 0, 2)

    def flat(value):
        return value.transpose(1, 0, 2).reshape(tok, -1)

    def first_group(owner):
        return owner * own // group_heads

    def pieces_for(owner):
        return (
            lax.dynamic_slice_in_dim(d, owner * width, width, 1),
            lax.dynamic_slice_in_dim(c, first_group(owner) * state_dim, span * state_dim, 1),
            by_group(lax.dynamic_slice_in_dim(wa, owner * own, own, 1), span),
        )

    def swap(value, k):
        return lax.ppermute(value, "resp", [(i, i ^ k) for i in range(count)])

    received = [pieces_for(me)]
    for k in range(1, count):
        received.append(tuple(swap(piece, k) for piece in pieces_for(me ^ k)))

    grad_b, grad_c, row_sum, col_sum = within(
        x, d, b, c, by_group(wa, groups), by_group(wb, groups), head_dim
    )
    codes = state_codes.reshape(width, state_dim)
    scale = state_scales.astype(F32).reshape(1, width)
    returned = []
    for k in range(count):
        d_c, d_l = carried(*received[k], codes, scale, head_dim)
        returned.append((d_c, d_l) if k == 0 else (swap(d_c, k), swap(d_l, k)))
    ds, cs, ws = zip(*received)
    grad_state = state_gradient(ds, cs, ws, head_dim).reshape(state_codes.shape)

    d_log = jnp.zeros((tok, all_heads), F32)
    for k in range(count):
        owner = me ^ k
        d_c, d_l = returned[k]
        first = first_group(owner) * state_dim
        held = lax.dynamic_slice_in_dim(grad_c, first, span * state_dim, 1)
        grad_c = lax.dynamic_update_slice_in_dim(grad_c, held + d_c, first, 1)
        d_log = lax.dynamic_update_slice_in_dim(d_log, flat(d_l), owner * own, 1)
    row_sum, col_sum = flat(row_sum), flat(col_sum)
    d_log = d_log + (row_sum - col_sum)
    later = jnp.dot(lower.T, d_log, precision=lax.Precision.HIGHEST)
    grad_dt = (col_sum / step - decay_rate[None, :] * later) * jax.nn.sigmoid(dt)
    return grad_state, grad_b[None], grad_c.astype(BF16)[None], grad_dt[None]


def solution(mesh):
    both = ("prompt", "resp")
    return jax.shard_map(
        functools.partial(per_device, mesh.shape["resp"]),
        mesh=mesh,
        in_specs=(
            P(both, None, None),
            P(both, None, None),
            P(both, None, None),
            P(both, None, None),
            P(both, None, None),
            P(),
            P(both, None, None),
            P(both, None),
            P(both),
            P(both),
            P(both),
        ),
        out_specs=(P(both, None, None),) * 4,
        check_vma=False,
    )
```

time: 449 us -> 127 us (0.28)
  waiting for transfers between devices: 219 us -> 0.04 us
  matrix products: 114 us -> 1.26 us
  Pallas kernels: 0 us -> 54.2 us
  other arithmetic: 37.3 us -> 8.95 us
  starting transfers between devices: 0.08 us -> 18.9 us
  loops' own time: 16.3 us -> 0 us
  between operations: 16.1 us -> 3.05 us
  blocking collectives: 9.85 us -> 0 us
  local copies, waits for them, and re-layouts: 34 us -> 39 us
    reduce_scatter x1 -> x0, waiting for transfers between devices: 151 us -> none  [per_device(): lax.psum_scatter(grad_part, 'resp', scatter_dimension=0, tiled=True)]
    dot_general x56 -> x2, matrix products: 114 us -> 1.26 us  [the longest x1 0.95 us: per_device(): later = jnp.dot(lower.T, d_log, precision=lax.Precision.HIGHEST)]
    all_gather x1 -> x0, waiting for transfers between devices: 67.3 us -> none  [per_device(): lax.all_gather(state_codes, 'resp', axis=0, tiled=True)]
    pallas_call x0 -> x6, Pallas kernels: none -> 54.2 us  [the longest x1 24.1 us: within(): pl.pallas_call(functools.partial(within_kernel, head_dim), grid=(groups,)...]
    mul x17 -> x0, other arithmetic: 20.3 us -> none  [the longest x1 10.2 us: per_device(): codes_all.astype(jnp.float32) * scales_all.astype(jnp.float32)[:, :, None]]
    ppermute x0 -> x15, starting transfers between devices: none -> 18.9 us  [swap(): return lax.ppermute(value, 'resp', [(i, i ^ k) for i in range(count)])]
    another operation x1 -> x0, loops' own time: 16.3 us -> none  [response_grads(): results = lax.map(one_group, jnp.arange(group_count, dtype=jnp.int32))]
    reshape x0 -> x13, local copies, waits for them, and re-layouts: none -> 11.1 us  [the longest x6 5.92 us: by_group(): return value.reshape(tok, pieces, -1).transpose(1, 0, 2)]
  transfers between devices with their start and end apart: 2 -> 15, of which waited for: 2 -> 0; matrix products, arithmetic and copies ran while one was open for 4% -> 30% of each run, Pallas kernels for 0% -> 43%
where the time goes in v1:
time: 127 us; the launch traced here: 125 us
  Pallas kernels  54.2 us (43%)
  local copies, waits for them, and re-layouts  39 us (31%)
  starting transfers between devices  18.9 us (15%)
  other arithmetic  8.95 us (7%)
  between operations  3.05 us (2%)
    pallas_call x1, Pallas kernels, within(): pl.pallas_call(functools.partial(within_kernel, head_dim), grid=(groups,)...  24.1 us
    ppermute x15, starting transfers between devices, swap(): return lax.ppermute(value, 'resp', [(i, i ^ k) for i in range(count)])  18.9 us
    pallas_call x4, Pallas kernels, carried(): pl.pallas_call(functools.partial(carried_kernel, head_dim), grid=(span,),...  17.8 us
    pallas_call x1, Pallas kernels, state_gradient(): pl.pallas_call(functools.partial(state_kernel, head_dim, count), grid=(wi...  12.4 us
    transpose x6, local copies, waits for them, and re-layouts, flat(): return value.transpose(1, 0, 2).reshape(tok, -1)  7.37 us
    dynamic_update_slice x4, other arithmetic, per_device(): grad_c = lax.dynamic_update_slice_in_dim(grad_c, held + d_c, first, 1)  6.86 us
    unnamed x34, local copies, waits for them, and re-layouts  6.31 us
    reshape x6, local copies, waits for them, and re-layouts, by_group(): return value.reshape(tok, pieces, -1).transpose(1, 0, 2)  5.92 us
  transfers between devices with their start and end apart: 15, of which 0 were waited for; matrix products, arithmetic and copies ran while one was open for 30% of the time, Pallas kernels for 43%

profile of v1, /device:TPU:0, one launch (start us, length us, event | category | flops | bytes accessed | tf_op | source)
XLA Modules:
  0.0 125.4 jit_solution(18004266942370898131)
XLA Ops:
  0.8 1.8 %dynamic-slice_bitcast_fusion.4 = (bf16[128,512]{1,0:T(8,128)(2,1)}, bf16[128,512]{1,0:T(8,128)(2,1)}, bf16[128,512]{1,0:T(8,128)(2,1)}, bf16[128,512]{1,0:T(8,128)(2,1)S(1)}) fusion(bf16[1,128,2048]{2,1,0:T(8,128)(2,1)} %param.14, s32[]{:T(128)S(6)} %select_n.89, s32[]{:T(128)S(6)} %select_n.87, s32[]{:T(128)S(6)} %select_n.85, s32[]{:T(128)S(6)} %select_n.83), kind=kLoop, calls=%fused_computation.29 | loop fusion | bytes 1048592 | tf_op jit(solution)/shard_map/dynamic_slice | solution.py:275
  2.6 2.9 %collective-permute-start.3 = (bf16[128,512]{1,0:T(8,128)(2,1)}, bf16[128,512]{1,0:T(8,128)(2,1)S(1)}, u32[]{:S(2)}, u32[]{:S(2)}) collective-permute-start(bf16[128,512]{1,0:T(8,128)(2,1)} %get-tuple-element.34), channel_id=1, source_target_pairs={{0,1},{1,0},{2,3},{3,2},{4,5},{5,4},{6,7},{7,6},{8,9},{9,8},{10,11... | collective-permute-start | bytes 393224 | tf_op jit(solution)/shard_map/ppermute | solution.py:280
  5.5 4.0 %dynamic-slice_bitcast_fusion = (bf16[128,4096]{1,0:T(8,128)(2,1)}, bf16[128,4096]{1,0:T(8,128)(2,1)}, bf16[128,4096]{1,0:T(8,128)(2,1)}, bf16[128,4096]{1,0:T(8,128)(2,1)S(1)}) fusion(bf16[1,128,16384]{2,1,0:T(8,128)(2,1)} %param.12, s32[]{:T(128)S(6)} %select_n.81, s32[]{:T(128)S(6)} %select_n.80, s32[]{:T(128)S(6)} %select_n.79, s32[]{:T(128)S(6)} %select_n.78), kind=kLoop, calls=%fused_computation.5 | loop fusion | bytes 8388624 | tf_op jit(solution)/shard_map/dynamic_slice | solution.py:274
  9.6 2.0 %collective-permute-start.1 = (bf16[128,4096]{1,0:T(8,128)(2,1)}, bf16[128,4096]{1,0:T(8,128)(2,1)}, u32[]{:S(2)}, u32[]{:S(2)}) collective-permute-start(bf16[128,4096]{1,0:T(8,128)(2,1)} %get-tuple-element.29), channel_id=1, source_target_pairs={{0,2},{1,3},{2,0},{3,1},{4,6},{5,7},{6,4},{7,5},{8,10},{9,11},{10,... | collective-permute-start | bytes 3145736 | tf_op jit(solution)/shard_map/ppermute | solution.py:280
  13.6 0.3 exponential_multiply_fusion
  14.0 0.8 constant_dynamic-slice_fusion
  14.8 0.1 copy.17
  14.9 0.8 copy.18
  15.6 1.5 %collective-permute-start.6 = (f32[2,128,32]{2,1,0:T(8,128)}, f32[2,128,32]{2,1,0:T(8,128)}, u32[]{:S(2)}, u32[]{:S(2)}) collective-permute-start(f32[2,128,32]{2,1,0:T(8,128)} %bitcast.14), channel_id=1, source_target_pairs={{0,1},{1,0},{2,3},{3,2},{4,5},{5,4},{6,7},{7,6},{8,9},{9,8},{10,11... | collective-permute-start | bytes 98312 | tf_op jit(solution)/shard_map/ppermute | solution.py:280
  17.1 0.1 copy.23
  17.2 0.1 reshape.94.scale_ref
  17.3 0.1 copy.15
  17.4 0.1 copy.16
  17.5 1.0 copy.24
  18.5 0.1 copy.25
  18.6 1.0 copy.26
  19.6 1.0 copy-done.3
  20.7 1.0 copy-done.4
  21.7 1.0 copy-done.5
  22.8 1.0 copy-done.7
  23.8 24.1 %within.1 = (bf16[128,2048]{1,0:T(8,128)(2,1)}, f32[128,2048]{1,0:T(8,128)}, f32[8,128,32]{2,1,0:T(8,128)S(1)}, f32[8,128,32]{2,1,0:T(8,128)S(1)}) custom-call(bf16[128,16384]{1,0:T(8,128)(2,1)} %bitcast.118, bf16[128,16384]{1,0:T(8,128)(2,1)} %bitcast.100, bf16[128,2048]{1,0:T(8,128)(2,1)S(1)} %bitcast.99, bf16[128,2048]{1,0:T(8,128)(2,1)S(1)} %bitcast.97, ...), custom_call_target="tpu_custom_call" | custom-call | flops 6442450944 | bytes 9961472 | tf_op jit(solution)/shard_map/within/pallas_call | solution.py:105
  47.9 0.8 copy-done.1
  48.7 0.8 copy-done.2
  49.5 3.3 %carried.4 = (f32[128,512]{1,0:T(8,128)S(1)}, f32[2,128,32]{2,1,0:T(8,128)S(1)}) custom-call(bf16[128,4096]{1,0:T(8,128)(2,1)S(1)} %get-tuple-element.31.refs_0_.d_ref, bf16[128,512]{1,0:T(8,128)(2,1)S(1)} %get-tuple-element.35.refs_4_.c_ref, f32[2,128,32]{2,1,0:T(8,128)S(1)} %bitcast.91, bf16[4096,256]{1,0:T(8,128)(2,1)S(1)} %bitcast.87, ...), custom_call_target="tpu_custom_call" | custom-call | flops 805306368 | bytes 3145728 | tf_op jit(solution)/shard_map/carried/pallas_call | solution.py:162
  52.8 2.1 %collective-permute-start.4 = (bf16[128,512]{1,0:T(8,128)(2,1)}, bf16[128,512]{1,0:T(8,128)(2,1)}, u32[]{:S(2)}, u32[]{:S(2)}) collective-permute-start(bf16[128,512]{1,0:T(8,128)(2,1)} %get-tuple-element.33), channel_id=1, source_target_pairs={{0,2},{1,3},{2,0},{3,1},{4,6},{5,7},{6,4},{7,5},{8,10},{9,11},{10,... | collective-permute-start | bytes 393224 | tf_op jit(solution)/shard_map/ppermute | solution.py:280
  54.9 1.7 %add_dynamic-update-slice_fusion.3 = f32[128,2048]{1,0:T(8,128)} fusion(f32[128,2048]{1,0:T(8,128)} %get-tuple-element.17, s32[]{:T(128)S(6)} %select_n.83, f32[128,512]{1,0:T(8,128)S(1)} %get-tuple-element.18), kind=kLoop, calls=%fused_computation.14 | loop fusion | flops 65536 | bytes 786436 | tf_op jit(solution)/shard_map/dynamic_update_slice | solution.py:304
  56.6 1.6 %copy.29 = f32[128,2,32]{0,2,1:T(8,128)} copy(f32[128,2,32]{2,0,1:T(8,128)} %bitcast.98) | data formatting | bytes 65536 | tf_op jit(solution)/shard_map/transpose | solution.py:267
  58.2 1.5 %copy.30 = f32[128,64]{1,0:T(8,128)} copy(f32[128,64]{0,1:T(8,128)} %bitcast.108) | data formatting | bytes 65536 | tf_op jit(solution)/shard_map/reshape | solution.py:267
  59.7 1.5 %copy.19 = f32[128,64]{0,1:T(8,128)} copy(f32[128,64]{1,0:T(8,128)} %get-tuple-element.39) | data formatting | bytes 65536 | tf_op jit(solution)/shard_map/dynamic_slice | solution.py:276
  61.2 1.5 %copy.20 = f32[128,2,32]{2,0,1:T(8,128)} copy(f32[128,2,32]{0,2,1:T(8,128)} %bitcast.109) | data formatting | bytes 65536 | tf_op jit(solution)/shard_map/reshape | solution.py:264
  62.7 1.5 %copy.21 = f32[128,64]{0,1:T(8,128)} copy(f32[128,64]{1,0:T(8,128)} %get-tuple-element.38) | data formatting | bytes 65536 | tf_op jit(solution)/shard_map/dynamic_slice | solution.py:276
  64.3 1.5 %copy.22 = f32[128,2,32]{2,0,1:T(8,128)} copy(f32[128,2,32]{0,2,1:T(8,128)} %bitcast.110) | data formatting | bytes 65536 | tf_op jit(solution)/shard_map/reshape | solution.py:264
  65.8 1.9 %copy.27 = f32[128,8,32]{0,2,1:T(8,128)} copy(f32[128,8,32]{2,0,1:T(8,128)} %bitcast.94) | data formatting | bytes 262144 | tf_op jit(solution)/shard_map/transpose | solution.py:267
  67.7 1.7 %copy.28 = f32[128,256]{1,0:T(8,128)} copy(f32[128,256]{0,1:T(8,128)} %bitcast.104) | data formatting | bytes 262144 | tf_op jit(solution)/shard_map/reshape | solution.py:267
  69.3 1.9 %copy.37 = f32[128,8,32]{0,2,1:T(8,128)} copy(f32[128,8,32]{2,0,1:T(8,128)} %bitcast.93) | data formatting | bytes 262144 | tf_op jit(solution)/shard_map/transpose | solution.py:267
  71.2 1.7 %copy.38 = f32[128,256]{1,0:T(8,128)} copy(f32[128,256]{0,1:T(8,128)} %bitcast.105) | data formatting | bytes 262144 | tf_op jit(solution)/shard_map/reshape | solution.py:267
  72.9 0.7 max.8
  73.6 1.6 %dynamic_update_slice.28 = f32[128,256]{1,0:T(8,128)} dynamic-update-slice(f32[128,256]{1,0:T(8,128)} %max.8, f32[128,64]{1,0:T(8,128)} %copy.30, s32[]{:T(128)} %constant.70.clone.1, s32[]{:T(128)S(6)} %select_n.92) | dynamic-update-slice | bytes 65540 | tf_op jit(solution)/shard_map/dynamic_update_slice | solution.py:305
  75.2 3.1 %collective-permute-start.5 = (bf16[128,512]{1,0:T(8,128)(2,1)}, bf16[128,512]{1,0:T(8,128)(2,1)S(1)}, u32[]{:S(2)}, u32[]{:S(2)}) collective-permute-start(bf16[128,512]{1,0:T(8,128)(2,1)} %get-tuple-element.32), channel_id=1, source_target_pairs={{0,3},{1,2},{2,1},{3,0},{4,7},{5,6},{6,5},{7,4},{8,11},{9,10},{10,... | collective-permute-start | bytes 393224 | tf_op jit(solution)/shard_map/ppermute | solution.py:280
  78.3 4.8 %carried.5 = (f32[128,512]{1,0:T(8,128)}, f32[2,128,32]{2,1,0:T(8,128)S(1)}) custom-call(bf16[128,4096]{1,0:T(8,128)(2,1)} %collective-permute-done.refs_1_.d_ref, bf16[128,512]{1,0:T(8,128)(2,1)S(1)} %collective-permute-done.3.refs_5_.c_ref, f32[2,128,32]{2,1,0:T(8,128)} %collective-permute-done.6.refs_9_.w_ref, bf16[4096,256]{1,0:T(8,128)(2,1)S(1)} %bitcast.88, ...), custom_call_target="tpu_custom_call" | custom-call | flops 805306368 | bytes 3145728 | tf_op jit(solution)/shard_map/carried/pallas_call | solution.py:162
  83.1 1.8 %collective-permute-start.12 = (f32[2,128,32]{2,1,0:T(8,128)S(1)}, f32[2,128,32]{2,1,0:T(8,128)S(1)}, u32[]{:S(2)}, u32[]{:S(2)}) collective-permute-start(f32[2,128,32]{2,1,0:T(8,128)S(1)} %get-tuple-element.24), channel_id=1, source_target_pairs={{0,1},{1,0},{2,3},{3,2},{4,5},{5,4},{6,7},{7,6},{8,9},{9,8},{10,11... | collective-permute-start | bytes 98312 | tf_op jit(solution)/shard_map/ppermute | solution.py:280
  85.0 4.8 %carried.6 = (f32[128,512]{1,0:T(8,128)}, f32[2,128,32]{2,1,0:T(8,128)}) custom-call(bf16[128,4096]{1,0:T(8,128)(2,1)} %collective-permute-done.1.refs_2_.d_ref, bf16[128,512]{1,0:T(8,128)(2,1)} %collective-permute-done.4.refs_6_.c_ref, f32[2,128,32]{2,1,0:T(8,128)S(1)} %collective-permute-done.7.refs_10_.w_ref, bf16[4096,256]{1,0:T(8,128)(2,1)S(1)} %bitcast.89, ...), custom_call_target="tpu_custom_call" | custom-call | flops 805306368 | bytes 3145728 | tf_op jit(solution)/shard_map/carried/pallas_call | solution.py:162
  89.8 1.7 %collective-permute-start.13 = (f32[2,128,32]{2,1,0:T(8,128)}, f32[2,128,32]{2,1,0:T(8,128)}, u32[]{:S(2)}, u32[]{:S(2)}) collective-permute-start(f32[2,128,32]{2,1,0:T(8,128)} %get-tuple-element.25), channel_id=1, source_target_pairs={{0,2},{1,3},{2,0},{3,1},{4,6},{5,7},{6,4},{7,5},{8,10},{9,11},{10,... | collective-permute-start | bytes 98312 | tf_op jit(solution)/shard_map/ppermute | solution.py:280
  91.5 4.9 %carried.7 = (f32[128,512]{1,0:T(8,128)}, f32[2,128,32]{2,1,0:T(8,128)}) custom-call(bf16[128,4096]{1,0:T(8,128)(2,1)} %collective-permute-done.2.refs_3_.d_ref, bf16[128,512]{1,0:T(8,128)(2,1)S(1)} %collective-permute-done.5.refs_7_.c_ref, f32[2,128,32]{2,1,0:T(8,128)S(1)} %collective-permute-done.8.refs_11_.w_ref, bf16[4096,256]{1,0:T(8,128)(2,1)S(1)} %bitcast.90, ...), custom_call_target="tpu_custom_call" | custom-call | flops 805306368 | bytes 3145728 | tf_op jit(solution)/shard_map/carried/pallas_call | solution.py:162
  96.3 0.1 collective-permute-start.14
  96.4 1.8 %collective-permute-start.9 = (f32[128,512]{1,0:T(8,128)}, f32[128,512]{1,0:T(8,128)S(1)}, u32[]{:S(2)}, u32[]{:S(2)}) collective-permute-start(f32[128,512]{1,0:T(8,128)} %get-tuple-element.19), channel_id=1, source_target_pairs={{0,1},{1,0},{2,3},{3,2},{4,5},{5,4},{6,7},{7,6},{8,9},{9,8},{10,11... | collective-permute-start | bytes 786440 | tf_op jit(solution)/shard_map/ppermute | solution.py:280
  98.2 1.7 %collective-permute-start.10 = (f32[128,512]{1,0:T(8,128)}, f32[128,512]{1,0:T(8,128)S(1)}, u32[]{:S(2)}, u32[]{:S(2)}) collective-permute-start(f32[128,512]{1,0:T(8,128)} %get-tuple-element.20), channel_id=1, source_target_pairs={{0,2},{1,3},{2,0},{3,1},{4,6},{5,7},{6,4},{7,5},{8,10},{9,11},{10,... | collective-permute-start | bytes 786440 | tf_op jit(solution)/shard_map/ppermute | solution.py:280
  99.9 12.4 %state_gradient.1 = f32[4096,256]{1,0:T(8,128)} custom-call(bf16[128,4096]{1,0:T(8,128)(2,1)S(1)} %get-tuple-element.31.refs_0_.d_ref, bf16[128,4096]{1,0:T(8,128)(2,1)} %collective-permute-done.refs_1_.d_ref, bf16[128,4096]{1,0:T(8,128)(2,1)} %collective-permute-done.1.refs_2_.d_ref, bf16[128,4096]{1,0:T(8,128)(2,1)} %collective-permute-done.2.refs_3_.d_ref, ...), custom_call_target="tpu_custom_call" | custom-call | flops 2147483648 | bytes 8388608 | tf_op jit(solution)/shard_map/state_gradient/pallas_call | solution.py:211
  112.3 0.1 collective-permute-start.11
  112.4 0.5 copy-done.8
  112.9 1.0 copy.31
  113.9 0.1 copy.32
  114.0 1.0 copy.33
  115.0 0.1 copy.34
  115.1 0.1 copy.35
  115.1 0.1 copy.36
  115.3 0.8 dynamic_update_slice.29
  116.1 0.4 dynamic_update_slice.30
  116.5 0.6 dynamic_update_slice.31
  117.2 0.9 fusion.2
  118.1 1.7 %add_dynamic-update-slice_fusion.2 = f32[128,2048]{1,0:T(8,128)} fusion(f32[128,2048]{1,0:T(8,128)} %add_dynamic-update-slice_fusion.3, s32[]{:T(128)S(6)} %select_n.85, f32[128,512]{1,0:T(8,128)S(1)} %collective-permute-done.9), kind=kLoop, calls=%fused_computation.13 | loop fusion | flops 65536 | bytes 786436 | tf_op jit(solution)/shard_map/dynamic_update_slice | solution.py:304
  119.9 1.7 %add_dynamic-update-slice_fusion.1 = f32[128,2048]{1,0:T(8,128)} fusion(f32[128,2048]{1,0:T(8,128)} %add_dynamic-update-slice_fusion.2, s32[]{:T(128)S(6)} %select_n.87, f32[128,512]{1,0:T(8,128)S(1)} %collective-permute-done.10), kind=kLoop, calls=%fused_computation.12 | loop fusion | flops 65536 | bytes 786436 | tf_op jit(solution)/shard_map/dynamic_update_slice | solution.py:304
  121.6 1.7 %add_dynamic-update-slice_fusion = f32[128,2048]{1,0:T(8,128)} fusion(f32[128,2048]{1,0:T(8,128)} %add_dynamic-update-slice_fusion.1, s32[]{:T(128)S(6)} %select_n.89, f32[128,512]{1,0:T(8,128)S(1)} %collective-permute-done.11), kind=kLoop, calls=%fused_computation.11 | loop fusion | flops 65536 | bytes 786436 | tf_op jit(solution)/shard_map/dynamic_update_slice | solution.py:304
  123.3 2.1 %convert_bitcast_fusion = bf16[1,128,2048]{2,1,0:T(8,128)(2,1)} fusion(f32[128,2048]{1,0:T(8,128)} %add_dynamic-update-slice_fusion), kind=kLoop, calls=%fused_computation.9 | loop fusion | flops 262144 | bytes 1572864 | tf_op jit(solution)/shard_map/broadcast_in_dim | solution.py:310
  (48 shorter events, 0.2 us)
Async XLA Ops:
  2.6 72.6 %collective-permute-start.3 = (bf16[128,512]{1,0:T(8,128)(2,1)}, bf16[128,512]{1,0:T(8,128)(2,1)S(1)}, u32[]{:S(2)}, u32[]{:S(2)}) collective-permute-start(bf16[128,512]{1,0:T(8,128)(2,1)} %get-tuple-element.34), channel_id=1, source_target_pairs={{0,1},{1,0},{2,3},{3,2},{4,5},{5,4},{6,7},{7,6},{8,9},{9,8},{10,11... | collective-permute-start | bytes 393224 | tf_op jit(solution)/shard_map/ppermute | solution.py:280
  5.5 8.0 %copy-start.13 = (f32[256]{0:T(256)S(1)}, f32[256]{0:T(256)}, u32[]{:S(2)}) copy-start(f32[256]{0:T(256)} %param.16) | copy-start | bytes 3076
  5.5 8.1 %copy-start.15 = (f32[1,128,256]{2,1,0:T(8,128)S(1)}, f32[1,128,256]{2,1,0:T(8,128)}, u32[]{:S(2)}) copy-start(f32[1,128,256]{2,1,0:T(8,128)} %param.15) | copy-start | bytes 393220
  5.5 11.7 %copy-start.12 = (bf16[64,64]{1,0:T(8,128)(2,1)S(1)}, bf16[64,64]{1,0:T(8,128)(2,1)}, u32[]{:S(2)}) copy-start(bf16[64,64]{1,0:T(8,128)(2,1)} %param.18) | copy-start | bytes 24580
  9.6 65.6 %collective-permute-start = (bf16[128,4096]{1,0:T(8,128)(2,1)}, bf16[128,4096]{1,0:T(8,128)(2,1)}, u32[]{:S(2)}, u32[]{:S(2)}) collective-permute-start(bf16[128,4096]{1,0:T(8,128)(2,1)} %get-tuple-element.30), channel_id=1, source_target_pairs={{0,1},{1,0},{2,3},{3,2},{4,5},{5,4},{6,7},{7,6},{8,9},{9,8},{10,11... | collective-permute-start | bytes 3145736 | tf_op jit(solution)/shard_map/ppermute | solution.py:280
  9.6 75.3 %collective-permute-start.1 = (bf16[128,4096]{1,0:T(8,128)(2,1)}, bf16[128,4096]{1,0:T(8,128)(2,1)}, u32[]{:S(2)}, u32[]{:S(2)}) collective-permute-start(bf16[128,4096]{1,0:T(8,128)(2,1)} %get-tuple-element.29), channel_id=1, source_target_pairs={{0,2},{1,3},{2,0},{3,1},{4,6},{5,7},{6,4},{7,5},{8,10},{9,11},{10,... | collective-permute-start | bytes 3145736 | tf_op jit(solution)/shard_map/ppermute | solution.py:280
  15.6 37.2 %collective-permute-start.6 = (f32[2,128,32]{2,1,0:T(8,128)}, f32[2,128,32]{2,1,0:T(8,128)}, u32[]{:S(2)}, u32[]{:S(2)}) collective-permute-start(f32[2,128,32]{2,1,0:T(8,128)} %bitcast.14), channel_id=1, source_target_pairs={{0,1},{1,0},{2,3},{3,2},{4,5},{5,4},{6,7},{7,6},{8,9},{9,8},{10,11... | collective-permute-start | bytes 98312 | tf_op jit(solution)/shard_map/ppermute | solution.py:280
  17.1 74.3 %collective-permute-start.2 = (bf16[128,4096]{1,0:T(8,128)(2,1)}, bf16[128,4096]{1,0:T(8,128)(2,1)}, u32[]{:S(2)}, u32[]{:S(2)}) collective-permute-start(bf16[128,4096]{1,0:T(8,128)(2,1)} %get-tuple-element.28), channel_id=1, source_target_pairs={{0,3},{1,2},{2,1},{3,0},{4,7},{5,6},{6,5},{7,4},{8,11},{9,10},{10,... | collective-permute-start | bytes 3145736 | tf_op jit(solution)/shard_map/ppermute | solution.py:280
  19.6 1.0 copy-start.3
  20.7 1.0 copy-start.4
  21.7 1.0 copy-start.5
  22.8 1.0 copy-start.7
  23.8 25.7 %copy-start = (bf16[64,64,256]{2,1,0:T(8,128)(2,1)S(1)}, bf16[64,64,256]{2,1,0:T(8,128)(2,1)}, u32[]{:S(2)}) copy-start(bf16[64,64,256]{2,1,0:T(8,128)(2,1)} %param.17) | copy-start | bytes 6291460
  47.9 0.8 copy-start.1
  48.7 0.8 copy-start.2
  52.8 3.8 %copy-start.6 = (f32[2,128,32]{2,1,0:T(8,128)}, f32[2,128,32]{2,1,0:T(8,128)S(1)}, u32[]{:S(2)}) copy-start(f32[2,128,32]{2,1,0:T(8,128)S(1)} %get-tuple-element.23) | copy-start | bytes 98308
  52.8 30.3 %collective-permute-start.4 = (bf16[128,512]{1,0:T(8,128)(2,1)}, bf16[128,512]{1,0:T(8,128)(2,1)}, u32[]{:S(2)}, u32[]{:S(2)}) collective-permute-start(bf16[128,512]{1,0:T(8,128)(2,1)} %get-tuple-element.33), channel_id=1, source_target_pairs={{0,2},{1,3},{2,0},{3,1},{4,6},{5,7},{6,4},{7,5},{8,10},{9,11},{10,... | collective-permute-start | bytes 393224 | tf_op jit(solution)/shard_map/ppermute | solution.py:280
  75.2 7.9 %collective-permute-start.7 = (f32[2,128,32]{2,1,0:T(8,128)}, f32[2,128,32]{2,1,0:T(8,128)S(1)}, u32[]{:S(2)}, u32[]{:S(2)}) collective-permute-start(f32[2,128,32]{2,1,0:T(8,128)} %bitcast.117), channel_id=1, source_target_pairs={{0,2},{1,3},{2,0},{3,1},{4,6},{5,7},{6,4},{7,5},{8,10},{9,11},{10,... | collective-permute-start | bytes 98312 | tf_op jit(solution)/shard_map/ppermute | solution.py:280
  75.2 16.3 %collective-permute-start.5 = (bf16[128,512]{1,0:T(8,128)(2,1)}, bf16[128,512]{1,0:T(8,128)(2,1)S(1)}, u32[]{:S(2)}, u32[]{:S(2)}) collective-permute-start(bf16[128,512]{1,0:T(8,128)(2,1)} %get-tuple-element.32), channel_id=1, source_target_pairs={{0,3},{1,2},{2,1},{3,0},{4,7},{5,6},{6,5},{7,4},{8,11},{9,10},{10,... | collective-permute-start | bytes 393224 | tf_op jit(solution)/shard_map/ppermute | solution.py:280
  83.1 8.3 %collective-permute-start.8 = (f32[2,128,32]{2,1,0:T(8,128)}, f32[2,128,32]{2,1,0:T(8,128)S(1)}, u32[]{:S(2)}, u32[]{:S(2)}) collective-permute-start(f32[2,128,32]{2,1,0:T(8,128)} %bitcast.115), channel_id=1, source_target_pairs={{0,3},{1,2},{2,1},{3,0},{4,7},{5,6},{6,5},{7,4},{8,11},{9,10},{10,... | collective-permute-start | bytes 98312 | tf_op jit(solution)/shard_map/ppermute | solution.py:280
  83.1 29.1 %collective-permute-start.12 = (f32[2,128,32]{2,1,0:T(8,128)S(1)}, f32[2,128,32]{2,1,0:T(8,128)S(1)}, u32[]{:S(2)}, u32[]{:S(2)}) collective-permute-start(f32[2,128,32]{2,1,0:T(8,128)S(1)} %get-tuple-element.24), channel_id=1, source_target_pairs={{0,1},{1,0},{2,3},{3,2},{4,5},{5,4},{6,7},{7,6},{8,9},{9,8},{10,11... | collective-permute-start | bytes 98312 | tf_op jit(solution)/shard_map/ppermute | solution.py:280
  89.8 24.2 %collective-permute-start.13 = (f32[2,128,32]{2,1,0:T(8,128)}, f32[2,128,32]{2,1,0:T(8,128)}, u32[]{:S(2)}, u32[]{:S(2)}) collective-permute-start(f32[2,128,32]{2,1,0:T(8,128)} %get-tuple-element.25), channel_id=1, source_target_pairs={{0,2},{1,3},{2,0},{3,1},{4,6},{5,7},{6,4},{7,5},{8,10},{9,11},{10,... | collective-permute-start | bytes 98312 | tf_op jit(solution)/shard_map/ppermute | solution.py:280
  96.3 18.8 %collective-permute-start.14 = (f32[2,128,32]{2,1,0:T(8,128)}, f32[2,128,32]{2,1,0:T(8,128)S(1)}, u32[]{:S(2)}, u32[]{:S(2)}) collective-permute-start(f32[2,128,32]{2,1,0:T(8,128)} %get-tuple-element.26), channel_id=1, source_target_pairs={{0,3},{1,2},{2,1},{3,0},{4,7},{5,6},{6,5},{7,4},{8,11},{9,10},{10,... | collective-permute-start | bytes 98312 | tf_op jit(solution)/shard_map/ppermute | solution.py:280
  96.4 21.7 %collective-permute-start.9 = (f32[128,512]{1,0:T(8,128)}, f32[128,512]{1,0:T(8,128)S(1)}, u32[]{:S(2)}, u32[]{:S(2)}) collective-permute-start(f32[128,512]{1,0:T(8,128)} %get-tuple-element.19), channel_id=1, source_target_pairs={{0,1},{1,0},{2,3},{3,2},{4,5},{5,4},{6,7},{7,6},{8,9},{9,8},{10,11... | collective-permute-start | bytes 786440 | tf_op jit(solution)/shard_map/ppermute | solution.py:280
  98.2 17.1 %copy-start.11 = (f32[128,256]{1,0:T(8,128)S(1)}, f32[128,256]{1,0:T(8,128)}, u32[]{:S(2)}) copy-start(f32[128,256]{1,0:T(8,128)} %dynamic_update_slice.28) | copy-start | bytes 393220
  98.2 19.0 %copy-start.9 = (f32[128,256]{1,0:T(8,128)S(1)}, f32[128,256]{1,0:T(8,128)}, u32[]{:S(2)}) copy-start(f32[128,256]{1,0:T(8,128)} %copy.28) | copy-start | bytes 393220
  98.2 19.0 %copy-start.10 = (f32[128,256]{1,0:T(8,128)S(1)}, f32[128,256]{1,0:T(8,128)}, u32[]{:S(2)}) copy-start(f32[128,256]{1,0:T(8,128)} %copy.38) | copy-start | bytes 393220
  98.2 19.0 %copy-start.14 = (f32[256]{0:T(256)S(1)}, f32[256]{0:T(256)}, u32[]{:S(2)}) copy-start(f32[256]{0:T(256)} %param.16) | copy-start | bytes 3076
  98.2 19.0 %copy-start.16 = (f32[1,128,256]{2,1,0:T(8,128)S(1)}, f32[1,128,256]{2,1,0:T(8,128)}, u32[]{:S(2)}) copy-start(f32[1,128,256]{2,1,0:T(8,128)} %param.15) | copy-start | bytes 393220
  98.2 21.7 %collective-permute-start.10 = (f32[128,512]{1,0:T(8,128)}, f32[128,512]{1,0:T(8,128)S(1)}, u32[]{:S(2)}, u32[]{:S(2)}) collective-permute-start(f32[128,512]{1,0:T(8,128)} %get-tuple-element.20), channel_id=1, source_target_pairs={{0,2},{1,3},{2,0},{3,1},{4,6},{5,7},{6,4},{7,5},{8,10},{9,11},{10,... | collective-permute-start | bytes 786440 | tf_op jit(solution)/shard_map/ppermute | solution.py:280
  112.3 0.7 copy-start.8
  112.3 9.3 %collective-permute-start.11 = (f32[128,512]{1,0:T(8,128)}, f32[128,512]{1,0:T(8,128)S(1)}, u32[]{:S(2)}, u32[]{:S(2)}) collective-permute-start(f32[128,512]{1,0:T(8,128)} %get-tuple-element.21), channel_id=1, source_target_pairs={{0,3},{1,2},{2,1},{3,0},{4,7},{5,6},{6,5},{7,4},{8,11},{9,10},{10,... | collective-permute-start | bytes 786440 | tf_op jit(solution)/shard_map/ppermute | solution.py:280

commit v2 on v0

v2 whole, which is shorter than its diff:
```python
import functools
import jax
import jax.numpy as jnp
from jax import lax
from jax.experimental import pallas as pl
from jax.experimental.pallas import tpu as pltpu
from jax.sharding import PartitionSpec as P

F32 = jnp.float32
BF16 = jnp.bfloat16
CHUNK = 512
VMEM_BYTES = 56 * 1024 * 1024


def dot(left, right):
    return lax.dot_general(left, right, (((1,), (0,)), ((), ())), preferred_element_type=F32)


def dot_nt(left, right):
    return lax.dot_general(left, right, (((1,), (1,)), ((), ())), preferred_element_type=F32)


def dot_tn(left, right):
    return lax.dot_general(left, right, (((0,), (0,)), ((), ())), preferred_element_type=F32)


def split(value):
    high = value.astype(BF16)
    return high, (value - high.astype(F32)).astype(BF16)


def three_rows(value):
    high = value.astype(BF16)
    middle, low = split(value - high.astype(F32))
    return jnp.concatenate([high, middle, low], axis=0)


def head_mask(heads, head_dim, start, width):
    row = lax.broadcasted_iota(jnp.int32, (heads, width), 0)
    col = lax.broadcasted_iota(jnp.int32, (heads, width), 1) + start
    first = row * head_dim
    return jnp.where((col >= first) & (col < first + head_dim), 1.0, 0.0).astype(BF16)


def spread(weights, mask):
    return dot_tn(three_rows(weights), jnp.concatenate([mask, mask, mask], axis=0))


def kernel(
    count,
    groups,
    head_dim,
    x_hbm,
    d_hbm,
    b_ref,
    c_ref,
    dt_ref,
    rate_ref,
    codes_hbm,
    scale_ref,
    sign_ref,
    adv_ref,
    length_ref,
    state_hbm,
    gb_ref,
    gc_ref,
    gdt_ref,
    x_ref,
    d_ref,
    codes_ref,
    state_ref,
    got_d,
    got_c,
    got_w,
    parts_ref,
    c_flip,
    out_dc,
    out_dl,
    got_dc,
    got_dl,
    wa_ref,
    wb_ref,
    row_ref,
    col_ref,
    log_ref,
    total_ref,
    load_sem,
    state_sem,
    d_send,
    d_recv,
    c_send,
    c_recv,
    w_send,
    w_recv,
    dc_send,
    dc_recv,
    dl_send,
    dl_recv,
):
    tok, all_heads = dt_ref.shape
    state_dim = b_ref.shape[1] // groups
    group_heads = all_heads // groups
    group_width = group_heads * head_dim
    own = all_heads // count
    width = own * head_dim
    span = max(1, own // group_heads)
    part = own // span
    part_width = part * head_dim
    me = lax.axis_index("resp")

    def other(k):
        return lax.rem(me + k + count, count)

    def first_group(owner):
        return owner * own // group_heads

    barrier = pltpu.get_barrier_semaphore()
    for k in range(1, count):
        pl.semaphore_signal(
            barrier, inc=1, device_id={"resp": other(k)}, device_id_type=pl.DeviceIdType.MESH
        )

    def columns(owner, s):
        return pl.ds(pl.multiple_of(owner * width + s * part_width, 128), part_width)

    loads = [
        pltpu.make_async_copy(x_hbm, x_ref, load_sem.at[0]),
        pltpu.make_async_copy(d_hbm, d_ref, load_sem.at[1]),
        pltpu.make_async_copy(codes_hbm, codes_ref, load_sem.at[2]),
        pltpu.make_async_copy(
            d_hbm.at[:, pl.ds(pl.multiple_of(me * width, 128), width)], got_d.at[0], load_sem.at[3]
        ),
    ]
    for load in loads:
        load.start()
    pl.semaphore_wait(barrier, count - 1)

    def remote(source, target, send, recv, k):
        return pltpu.make_async_remote_copy(
            src_ref=source,
            dst_ref=target,
            send_sem=send,
            recv_sem=recv,
            device_id={"resp": other(k)},
            device_id_type=pl.DeviceIdType.MESH,
        )

    def send_d(k, s):
        return remote(
            d_hbm.at[:, columns(other(k), s)],
            got_d.at[k, :, pl.ds(s * part_width, part_width)],
            d_send.at[k, s],
            d_recv.at[k, s],
            k,
        )

    def state_columns(owner):
        return pl.ds(pl.multiple_of(first_group(owner) * state_dim, 128), span * state_dim)

    def heads_of(owner):
        return pl.ds(pl.multiple_of(owner * own, 8), own)

    def send_c(k):
        return remote(
            c_ref.at[:, state_columns(other(k))], got_c.at[k], c_send.at[k], c_recv.at[k], k
        )

    def send_w(k):
        return remote(wa_ref.at[heads_of(other(k)), :], got_w.at[k], w_send.at[k], w_recv.at[k], k)

    for k in range(1, count):
        send_d(k, 0).start()

    at = lax.broadcasted_iota(jnp.int32, (tok, tok), 0)
    of = lax.broadcasted_iota(jnp.int32, (tok, tok), 1)
    causal = at >= of
    lower = jnp.where(causal, 1.0, 0.0).astype(BF16)
    upper = jnp.where(at <= of, 1.0, 0.0).astype(BF16)
    dt = dt_ref[...]
    step = jnp.maximum(dt, 0.0) + jnp.log1p(jnp.exp(-jnp.abs(dt)))
    rate = rate_ref[...]
    log_decay = -rate * dot(jnp.concatenate([lower] * 3, axis=1), three_rows(step))
    sign = 2.0 * jnp.full((tok, 1), sign_ref[0], jnp.int32).astype(F32) - 1.0
    length = jnp.full((tok, 1), length_ref[0], jnp.int32)
    coefficient = sign * adv_ref[0] / length.astype(F32)
    row_coef = jnp.where(lax.broadcasted_iota(jnp.int32, (tok, 1), 0) < length, coefficient, 0.0)
    wa_ref[...] = (row_coef * jnp.exp(log_decay)).T
    wb_ref[...] = (step * jnp.exp(-log_decay)).T

    for k in range(1, count):
        send_w(k).start()
        send_c(k).start()
    for s in range(1, span):
        for k in range(1, count):
            send_d(k, s).start()
    got_c[0] = c_ref[:, state_columns(me)]
    got_w[0] = wa_ref[heads_of(me), :]
    loads[0].wait()
    loads[1].wait()

    chunk = min(CHUNK, group_width)

    def one_group(g, carry):
        states = pl.ds(pl.multiple_of(g * state_dim, 128), state_dim)
        heads = pl.ds(pl.multiple_of(g * group_heads, 8), group_heads)
        b = b_ref[:, states]
        c = c_ref[:, states]
        s_hi, s_lo = split(jnp.where(causal, dot_nt(c, b), 0.0))
        scores = jnp.concatenate([s_hi, s_lo, s_hi], axis=1)
        t_hi, t_lo = split(jnp.where(at <= of, dot_nt(b, c), 0.0))
        flipped = jnp.concatenate([t_hi, t_lo, t_hi], axis=1)
        wa = wa_ref[heads, :]
        wb = wb_ref[heads, :]
        d_scores = jnp.zeros((2 * tok, 2 * tok), F32)
        sums = jnp.zeros((group_heads, 4 * tok), F32)
        for start in range(0, group_width, chunk):
            here = pl.ds(pl.multiple_of(g * group_width + start, 128), chunk)
            mask = head_mask(group_heads, head_dim, start, chunk)
            w = d_ref[:, here].astype(F32) * spread(wa, mask)
            x = x_ref[:, here].astype(F32) * spread(wb, mask)
            w_hi, w_lo = split(w)
            x_hi, x_lo = split(x)
            d_scores += dot_nt(
                jnp.concatenate([w_hi, w_lo], axis=0), jnp.concatenate([x_hi, x_lo], axis=0)
            )
            p = w * dot(scores, jnp.concatenate([x_hi, x_hi, x_lo], axis=0))
            q = x * dot(flipped, jnp.concatenate([w_hi, w_hi, w_lo], axis=0))
            sums += dot_nt(mask, jnp.concatenate(split(p) + split(q), axis=0))
        row_ref[heads, :] = sums[:, :tok] + sums[:, tok : 2 * tok]
        col_ref[heads, :] = sums[:, 2 * tok : 3 * tok] + sums[:, 3 * tok :]
        d_scores = d_scores[:tok] + d_scores[tok:]
        d_scores = jnp.where(causal, d_scores[:, :tok] + d_scores[:, tok:], 0.0)
        total_ref[:, states] = dot(
            jnp.concatenate(split(d_scores), axis=1), jnp.concatenate([b, b], axis=0)
        )
        gb_ref[:, states] = dot(
            jnp.concatenate(split(d_scores.T), axis=1), jnp.concatenate([c, c], axis=0)
        ).astype(BF16)
        return carry

    lax.fori_loop(0, groups, one_group, 0)

    loads[2].wait()
    loads[3].wait()
    chunk = min(CHUNK, part_width)

    def back_dc(k, s):
        return remote(
            out_dc.at[k, :, pl.ds(s * state_dim, state_dim)],
            got_dc.at[k, :, pl.ds(s * state_dim, state_dim)],
            dc_send.at[k, s],
            dc_recv.at[k, s],
            -k,
        )

    def back_dl(k, s):
        return remote(
            out_dl.at[k, pl.ds(s * part, part), :],
            got_dl.at[k, pl.ds(s * part, part), :],
            dl_send.at[k, s],
            dl_recv.at[k, s],
            -k,
        )

    writes = []
    for s in range(span):

        def one_response(k, carry, s=s):
            @pl.when(k > 0)
            def _():
                if s == 0:
                    send_w(k).wait_recv()
                    send_c(k).wait_recv()
                send_d(k, s).wait_recv()

            c = got_c[k, :, s * state_dim : (s + 1) * state_dim]
            w = got_w[k, s * part : (s + 1) * part, :]
            rows = pl.ds(pl.multiple_of(k * 2 * tok, 2 * tok), 2 * tok)
            d_c = jnp.zeros((2 * tok, state_dim), F32)
            sums = jnp.zeros((part, 2 * tok), F32)
            for start in range(0, part_width, chunk):
                here = slice(s * part_width + start, s * part_width + start + chunk)
                codes = codes_ref[here, :]
                mask = head_mask(part, head_dim, start, chunk)
                v = got_d[k, :, here].astype(F32) * spread(w, mask) * scale_ref[:, here]
                halves = jnp.concatenate(split(v), axis=0)
                parts_ref[rows, start : start + chunk] = halves
                d_c += dot(halves, codes)
                p = v * dot_nt(c, codes)
                sums += dot_nt(mask, jnp.concatenate(split(p), axis=0))
            out_dc[k, :, s * state_dim : (s + 1) * state_dim] = d_c[:tok] + d_c[tok:]
            out_dl[k, s * part : (s + 1) * part, :] = sums[:, :tok] + sums[:, tok:]

            @pl.when(k > 0)
            def _():
                back_dc(k, s).start()
                back_dl(k, s).start()

            flip = c.T
            c_flip[k] = jnp.concatenate([flip, flip], axis=1)
            return carry

        lax.fori_loop(0, count, one_response, 0)

        def one_chunk(j, carry, s=s):
            here = pl.ds(pl.multiple_of(j * chunk, 128), chunk)
            total = jnp.zeros((state_dim, chunk), F32)
            for k in range(count):
                total += dot(c_flip[k], parts_ref[k * 2 * tok : (k + 1) * 2 * tok, here])
            start = pl.multiple_of(s * part_width + j * chunk, 128)
            total = total / scale_ref[:, pl.ds(start, chunk)]
            state_ref[pl.ds(start, chunk), :] = total.T
            return carry

        lax.fori_loop(0, part_width // chunk, one_chunk, 0)
        rows = pl.ds(s * part_width, part_width)
        write = pltpu.make_async_copy(state_ref.at[rows, :], state_hbm.at[rows, :], state_sem.at[s])
        write.start()
        writes.append(write)

    def add_back(owner, d_c, d_l):
        states = state_columns(owner)
        total_ref[:, states] = total_ref[:, states] + d_c
        log_ref[heads_of(owner), :] = d_l

    add_back(me, out_dc[0], out_dl[0])
    for k in range(1, count):
        for s in range(span):
            back_dc(k, s).wait_recv()
            back_dl(k, s).wait_recv()
        add_back(other(k), got_dc[k], got_dl[k])
    gc_ref[...] = total_ref[...].astype(BF16)
    col = col_ref[...]
    d_log = (log_ref[...] + (row_ref[...] - col)).T
    later = dot(jnp.concatenate([upper] * 3, axis=1), three_rows(d_log))
    gdt_ref[...] = (col.T / step - rate * later) / (1.0 + jnp.exp(-dt))

    for k in range(1, count):
        send_w(k).wait_send()
        send_c(k).wait_send()
        for s in range(span):
            send_d(k, s).wait_send()
            back_dc(k, s).wait_send()
            back_dl(k, s).wait_send()
    for write in writes:
        write.wait()


def per_device(
    count,
    inputs,
    cotangent,
    b_proj,
    c_proj,
    dt_raw,
    decay_rate,
    state_codes,
    state_scales,
    sign_bucket,
    adv_scale,
    lengths,
):
    x, d, b, c, dt = inputs[0], cotangent[0], b_proj[0], c_proj[0], dt_raw[0]
    tok, all_heads = dt.shape
    own, head_dim, state_dim = state_codes.shape
    groups = b.shape[1] // state_dim
    span = max(1, own * groups // all_heads)
    part = own // span
    width = own * head_dim
    whole = pl.BlockSpec(memory_space=pltpu.VMEM)
    there = pl.BlockSpec(memory_space=pl.ANY)
    scalar = pl.BlockSpec(memory_space=pltpu.SMEM)
    dma = pltpu.SemaphoreType.DMA
    flops = 24 * tok * tok * x.shape[1] + 12 * count * tok * width * state_dim
    grad_state, grad_b, grad_c, grad_dt = pl.pallas_call(
        functools.partial(kernel, count, groups, head_dim),
        in_specs=[there, there, whole, whole, whole, whole, there, whole, scalar, scalar, scalar],
        out_specs=[there, whole, whole, whole],
        out_shape=[
            jax.ShapeDtypeStruct((width, state_dim), F32),
            jax.ShapeDtypeStruct(b.shape, BF16),
            jax.ShapeDtypeStruct(c.shape, BF16),
            jax.ShapeDtypeStruct(dt.shape, F32),
        ],
        scratch_shapes=[
            pltpu.VMEM(x.shape, BF16),
            pltpu.VMEM(d.shape, BF16),
            pltpu.VMEM((width, state_dim), BF16),
            pltpu.VMEM((width, state_dim), F32),
            pltpu.VMEM((count, tok, width), BF16),
            pltpu.VMEM((count, tok, span * state_dim), BF16),
            pltpu.VMEM((count, own, tok), F32),
            pltpu.VMEM((count * 2 * tok, part * head_dim), BF16),
            pltpu.VMEM((count, state_dim, 2 * tok), BF16),
            pltpu.VMEM((count, tok, span * state_dim), F32),
            pltpu.VMEM((count, own, tok), F32),
            pltpu.VMEM((count, tok, span * state_dim), F32),
            pltpu.VMEM((count, own, tok), F32),
        ]
        + [pltpu.VMEM((all_heads, tok), F32)] * 5
        + [pltpu.VMEM(c.shape, F32), dma((4,)), dma((span,))]
        + [dma((count, span))] * 2
        + [dma((count,))] * 4
        + [dma((count, span))] * 4,
        compiler_params=pltpu.CompilerParams(
            collective_id=0, has_side_effects=True, vmem_limit_bytes=VMEM_BYTES
        ),
        cost_estimate=pl.CostEstimate(
            flops=flops, bytes_accessed=4 * x.size + 8 * width * state_dim, transcendentals=0
        ),
        name="scan_backward",
    )(
        x,
        d,
        b,
        c,
        dt,
        decay_rate.reshape(1, all_heads),
        state_codes.reshape(width, state_dim),
        state_scales.astype(F32).reshape(1, width),
        sign_bucket,
        adv_scale,
        lengths,
    )
    return grad_state.reshape(state_codes.shape), grad_b[None], grad_c[None], grad_dt[None]


def solution(mesh):
    both = ("prompt", "resp")
    return jax.shard_map(
        functools.partial(per_device, mesh.shape["resp"]),
        mesh=mesh,
        in_specs=(
            P(both, None, None),
            P(both, None, None),
            P(both, None, None),
            P(both, None, None),
            P(both, None, None),
            P(),
            P(both, None, None),
            P(both, None),
            P(both),
            P(both),
            P(both),
        ),
        out_specs=(P(both, None, None),) * 4,
        check_vma=False,
    )
```

time: 449 us -> 84.4 us (0.19)
  waiting for transfers between devices: 219 us -> 0 us
  matrix products: 114 us -> 0 us
  Pallas kernels: 0 us -> 73 us
  other arithmetic: 37.3 us -> 0 us
  local copies, waits for them, and re-layouts: 34 us -> 8.46 us
  loops' own time: 16.3 us -> 0 us
  between operations: 16.1 us -> 2.6 us
  blocking collectives: 9.85 us -> 0 us
    reduce_scatter x1 -> x0, waiting for transfers between devices: 151 us -> none  [per_device(): lax.psum_scatter(grad_part, 'resp', scatter_dimension=0, tiled=True)]
    dot_general x56 -> x0, matrix products: 114 us -> none  [the longest x24 67.7 us: group_forward(): jnp.einsum('tn,hpn->thp', group_c, group_state, precision=lax.Precision.H...]
    pallas_call x0 -> x1, Pallas kernels: none -> 73 us  [per_device(): pl.pallas_call(functools.partial(kernel, count, groups, head_dim), in_spe...]
    all_gather x1 -> x0, waiting for transfers between devices: 67.3 us -> none  [per_device(): lax.all_gather(state_codes, 'resp', axis=0, tiled=True)]
    mul x17 -> x0, other arithmetic: 20.3 us -> none  [the longest x1 10.2 us: per_device(): codes_all.astype(jnp.float32) * scales_all.astype(jnp.float32)[:, :, None]]
    another operation x1 -> x0, loops' own time: 16.3 us -> none  [response_grads(): results = lax.map(one_group, jnp.arange(group_count, dtype=jnp.int32))]
    dynamic_slice x24 -> x0, local copies, waits for them, and re-layouts: 14.1 us -> none  [the longest x8 8.82 us: one_group(): lax.dynamic_slice_in_dim(x_rows, group_idx * group_width, group_width, 1)]
    another operation x18 -> x0, other arithmetic: 10.4 us -> none  [the longest x16 10.4 us: group_forward(): log_decay = jnp.cumsum(-step_size * group_rate[None, :], axis=0)]
  transfers between devices with their start and end apart: 2 -> 0, of which waited for: 2 -> 0; matrix products, arithmetic and copies ran while one was open for 4% -> 0% of each run, Pallas kernels for 0% -> 0%
where the time goes in v2:
time: 84.4 us; the launch traced here: 84.1 us
  Pallas kernels  73 us (86%)
  local copies, waits for them, and re-layouts  8.46 us (10%)
  between operations  2.6 us (3%)
    pallas_call x1, Pallas kernels, per_device(): pl.pallas_call(functools.partial(kernel, count, groups, head_dim), in_spe...  73 us
    unnamed x10, local copies, waits for them, and re-layouts  7.04 us

profile of v2, /device:TPU:0, one launch (start us, length us, event | category | flops | bytes accessed | tf_op | source)
XLA Modules:
  0.0 84.1 jit_solution(4736913973744851573)
XLA Ops:
  2.6 1.4 %reshape.28.scale_ref = f32[1,4096]{1,0:T(1,128)} reshape(bf16[64,64]{1,0:T(8,128)(2,1)} %param.18) | data formatting | bytes 24576 | tf_op jit(solution)/shard_map/reshape | solution.py:420
  4.0 73.0 %scan_backward.1 = (f32[4096,256]{1,0:T(8,128)}, bf16[128,2048]{1,0:T(8,128)(2,1)}, bf16[128,2048]{1,0:T(8,128)(2,1)}, f32[128,256]{1,0:T(8,128)}) custom-call(bf16[128,16384]{1,0:T(8,128)(2,1)} %bitcast.15, bf16[128,16384]{1,0:T(8,128)(2,1)} %bitcast.16, bf16[128,2048]{1,0:T(8,128)(2,1)} %bitcast.18, bf16[128,2048]{1,0:T(8,128)(2,1)} %bitcast.19, ...), custom_call_target="tpu_custom_call" | custom-call | flops 12884901888 | bytes 16777216 | tf_op jit(solution)/shard_map/scan_backward/pallas_call | solution.py:375
  77.0 0.0 copy-start.1
  77.0 0.0 copy-start
  77.1 0.0 copy-start.2
  77.1 4.8 %copy.22 = f32[64,64,256]{2,1,0:T(8,128)} copy(f32[64,64,256]{2,1,0:T(8,128)} %bitcast.11) | data formatting | bytes 8388608
  81.9 0.0 copy-done.1
  81.9 0.8 copy.23
  82.7 0.0 copy-done
  82.7 0.8 copy.24
  83.5 0.0 copy-done.2
  83.5 0.7 copy.25
Async XLA Ops:
  77.0 4.8 %copy-start.1 = (bf16[128,2048]{1,0:T(8,128)(2,1)S(1)}, bf16[128,2048]{1,0:T(8,128)(2,1)}, u32[]{:S(2)}) copy-start(bf16[128,2048]{1,0:T(8,128)(2,1)} %get-tuple-element.9) | copy-start | bytes 1572868
  77.0 5.6 %copy-start = (bf16[128,2048]{1,0:T(8,128)(2,1)S(1)}, bf16[128,2048]{1,0:T(8,128)(2,1)}, u32[]{:S(2)}) copy-start(bf16[128,2048]{1,0:T(8,128)(2,1)} %get-tuple-element.10) | copy-start | bytes 1572868
  77.1 6.4 %copy-start.2 = (f32[128,256]{1,0:T(8,128)S(1)}, f32[128,256]{1,0:T(8,128)}, u32[]{:S(2)}) copy-start(f32[128,256]{1,0:T(8,128)} %get-tuple-element.11) | copy-start | bytes 393220

commit v3 on v2

--- a/solution.py
+++ b/solution.py
@@ -35,15 +35,14 @@
     return jnp.concatenate([high, middle, low], axis=0)
 
 
-def head_mask(heads, head_dim, start, width):
-    row = lax.broadcasted_iota(jnp.int32, (heads, width), 0)
-    col = lax.broadcasted_iota(jnp.int32, (heads, width), 1) + start
-    first = row * head_dim
-    return jnp.where((col >= first) & (col < first + head_dim), 1.0, 0.0).astype(BF16)
-
-
-def spread(weights, mask):
-    return dot_tn(three_rows(weights), jnp.concatenate([mask, mask, mask], axis=0))
+def over_rows(weights, head_dim):
+    heads, tok = weights.shape
+    return jnp.broadcast_to(weights[:, None, :], (heads, head_dim, tok)).reshape(-1, tok)
+
+
+def head_sums(value, head_dim):
+    rows, tok = value.shape
+    return jnp.sum(value.reshape(rows // head_dim, head_dim, tok), axis=1)
 
 
 def kernel(
@@ -73,7 +72,9 @@
     got_c,
     got_w,
     parts_ref,
-    c_flip,
+    c_twice,
+    codes_flip,
+    scale_rows,
     out_dc,
     out_dl,
     got_dc,
@@ -199,35 +200,35 @@
     loads[1].wait()
 
     chunk = min(CHUNK, group_width)
+    chunk_heads = chunk // head_dim
+    nothing = jnp.zeros((tok, tok), BF16)
+
+    def paired(high, low):
+        return jnp.concatenate(
+            [jnp.concatenate([high, low], axis=1), jnp.concatenate([high, nothing], axis=1)], axis=0
+        )
 
     def one_group(g, carry):
         states = pl.ds(pl.multiple_of(g * state_dim, 128), state_dim)
-        heads = pl.ds(pl.multiple_of(g * group_heads, 8), group_heads)
         b = b_ref[:, states]
         c = c_ref[:, states]
-        s_hi, s_lo = split(jnp.where(causal, dot_nt(c, b), 0.0))
-        scores = jnp.concatenate([s_hi, s_lo, s_hi], axis=1)
-        t_hi, t_lo = split(jnp.where(at <= of, dot_nt(b, c), 0.0))
-        flipped = jnp.concatenate([t_hi, t_lo, t_hi], axis=1)
-        wa = wa_ref[heads, :]
-        wb = wb_ref[heads, :]
+        scores = paired(*split(jnp.where(causal, dot_nt(c, b), 0.0)))
+        flipped = paired(*split(jnp.where(at <= of, dot_nt(b, c), 0.0)))
         d_scores = jnp.zeros((2 * tok, 2 * tok), F32)
-        sums = jnp.zeros((group_heads, 4 * tok), F32)
         for start in range(0, group_width, chunk):
             here = pl.ds(pl.multiple_of(g * group_width + start, 128), chunk)
-            mask = head_mask(group_heads, head_dim, start, chunk)
-            w = d_ref[:, here].astype(F32) * spread(wa, mask)
-            x = x_ref[:, here].astype(F32) * spread(wb, mask)
-            w_hi, w_lo = split(w)
-            x_hi, x_lo = split(x)
-            d_scores += dot_nt(
-                jnp.concatenate([w_hi, w_lo], axis=0), jnp.concatenate([x_hi, x_lo], axis=0)
+            heads = pl.ds(
+                pl.multiple_of(g * group_heads + start // head_dim, chunk_heads), chunk_heads
             )
-            p = w * dot(scores, jnp.concatenate([x_hi, x_hi, x_lo], axis=0))
-            q = x * dot(flipped, jnp.concatenate([w_hi, w_hi, w_lo], axis=0))
-            sums += dot_nt(mask, jnp.concatenate(split(p) + split(q), axis=0))
-        row_ref[heads, :] = sums[:, :tok] + sums[:, tok : 2 * tok]
-        col_ref[heads, :] = sums[:, 2 * tok : 3 * tok] + sums[:, 3 * tok :]
+            w = d_ref[:, here].T.astype(F32) * over_rows(wa_ref[heads, :], head_dim)
+            x = x_ref[:, here].T.astype(F32) * over_rows(wb_ref[heads, :], head_dim)
+            w_parts = jnp.concatenate(split(w), axis=1)
+            x_parts = jnp.concatenate(split(x), axis=1)
+            d_scores += dot_tn(w_parts, x_parts)
+            y = dot(x_parts, flipped)
+            u = dot(w_parts, scores)
+            row_ref[heads, :] = head_sums(w * (y[:, :tok] + y[:, tok:]), head_dim)
+            col_ref[heads, :] = head_sums(x * (u[:, :tok] + u[:, tok:]), head_dim)
         d_scores = d_scores[:tok] + d_scores[tok:]
         d_scores = jnp.where(causal, d_scores[:, :tok] + d_scores[:, tok:], 0.0)
         total_ref[:, states] = dot(
@@ -243,6 +244,14 @@
     loads[2].wait()
     loads[3].wait()
     chunk = min(CHUNK, part_width)
+    chunk_heads = chunk // head_dim
+    scales = scale_ref[...].astype(F32).T
+    for h in range(own):
+        scale_rows[h * head_dim : (h + 1) * head_dim, :] = jnp.broadcast_to(
+            scales[:, h : h + 1], (head_dim, tok)
+        )
+    for start in range(0, width, chunk):
+        codes_flip[:, start : start + chunk] = codes_ref[start : start + chunk, :].T
 
     def back_dc(k, s):
         return remote(
@@ -273,43 +282,38 @@
                     send_c(k).wait_recv()
                 send_d(k, s).wait_recv()
 
+            lanes = pl.ds(pl.multiple_of(k * 2 * tok, 128), 2 * tok)
             c = got_c[k, :, s * state_dim : (s + 1) * state_dim]
-            w = got_w[k, s * part : (s + 1) * part, :]
-            rows = pl.ds(pl.multiple_of(k * 2 * tok, 2 * tok), 2 * tok)
-            d_c = jnp.zeros((2 * tok, state_dim), F32)
-            sums = jnp.zeros((part, 2 * tok), F32)
+            c_flip = c.T
+            d_c = jnp.zeros((state_dim, 2 * tok), F32)
             for start in range(0, part_width, chunk):
                 here = slice(s * part_width + start, s * part_width + start + chunk)
-                codes = codes_ref[here, :]
-                mask = head_mask(part, head_dim, start, chunk)
-                v = got_d[k, :, here].astype(F32) * spread(w, mask) * scale_ref[:, here]
-                halves = jnp.concatenate(split(v), axis=0)
-                parts_ref[rows, start : start + chunk] = halves
-                d_c += dot(halves, codes)
-                p = v * dot_nt(c, codes)
-                sums += dot_nt(mask, jnp.concatenate(split(p), axis=0))
-            out_dc[k, :, s * state_dim : (s + 1) * state_dim] = d_c[:tok] + d_c[tok:]
-            out_dl[k, s * part : (s + 1) * part, :] = sums[:, :tok] + sums[:, tok:]
+                first = s * part + start // head_dim
+                heads = slice(first, first + chunk_heads)
+                v = got_d[k, :, here].T.astype(F32) * over_rows(got_w[k, heads, :], head_dim)
+                v = v * scale_rows[here, :]
+                v_parts = jnp.concatenate(split(v), axis=1)
+                parts_ref[start : start + chunk, lanes] = v_parts
+                d_c += dot(codes_flip[:, here], v_parts)
+                out_dl[k, heads, :] = head_sums(v * dot(codes_ref[here, :], c_flip), head_dim)
+            out_dc[k, :, s * state_dim : (s + 1) * state_dim] = (d_c[:, :tok] + d_c[:, tok:]).T
 
             @pl.when(k > 0)
             def _():
                 back_dc(k, s).start()
                 back_dl(k, s).start()
 
-            flip = c.T
-            c_flip[k] = jnp.concatenate([flip, flip], axis=1)
+            c_twice[lanes, :] = jnp.concatenate([c, c], axis=0)
             return carry
 
         lax.fori_loop(0, count, one_response, 0)
 
         def one_chunk(j, carry, s=s):
-            here = pl.ds(pl.multiple_of(j * chunk, 128), chunk)
-            total = jnp.zeros((state_dim, chunk), F32)
-            for k in range(count):
-                total += dot(c_flip[k], parts_ref[k * 2 * tok : (k + 1) * 2 * tok, here])
-            start = pl.multiple_of(s * part_width + j * chunk, 128)
-            total = total / scale_ref[:, pl.ds(start, chunk)]
-            state_ref[pl.ds(start, chunk), :] = total.T
+            rows = pl.ds(pl.multiple_of(j * chunk, chunk), chunk)
+            here = pl.ds(pl.multiple_of(s * part_width + j * chunk, chunk), chunk)
+            inverse = 1.0 / scale_rows[here, :]
+            wide = jnp.concatenate([inverse] * (state_dim // tok), axis=1)
+            state_ref[here, :] = dot(parts_ref[rows, :], c_twice[...]) * wide
             return carry
 
         lax.fori_loop(0, part_width // chunk, one_chunk, 0)
@@ -390,8 +394,10 @@
             pltpu.VMEM((count, tok, width), BF16),
             pltpu.VMEM((count, tok, span * state_dim), BF16),
             pltpu.VMEM((count, own, tok), F32),
-            pltpu.VMEM((count * 2 * tok, part * head_dim), BF16),
-            pltpu.VMEM((count, state_dim, 2 * tok), BF16),
+            pltpu.VMEM((part * head_dim, count * 2 * tok), BF16),
+            pltpu.VMEM((count * 2 * tok, state_dim), BF16),
+            pltpu.VMEM((state_dim, width), BF16),
+            pltpu.VMEM((width, tok), F32),
             pltpu.VMEM((count, tok, span * state_dim), F32),
             pltpu.VMEM((count, own, tok), F32),
             pltpu.VMEM((count, tok, span * state_dim), F32),
@@ -417,7 +423,7 @@
         dt,
         decay_rate.reshape(1, all_heads),
         state_codes.reshape(width, state_dim),
-        state_scales.astype(F32).reshape(1, width),
+        state_scales,
         sign_bucket,
         adv_scale,
         lengths,

time: 84.4 us -> 82.9 us (0.982)
  local copies, waits for them, and re-layouts: 8.46 us -> 7.04 us
    reshape x1 -> x0, local copies, waits for them, and re-layouts: 1.41 us -> none  [per_device(): state_scales.astype(F32).reshape(1, width)]
where the time goes in v3:
time: 82.9 us; the launch traced here: 82.7 us
  Pallas kernels  73.1 us (88%)
  local copies, waits for them, and re-layouts  7.04 us (8%)
  between operations  2.61 us (3%)
    pallas_call x1, Pallas kernels, per_device(): pl.pallas_call(functools.partial(kernel, count, groups, head_dim), in_spe...  73.1 us
    unnamed x10, local copies, waits for them, and re-layouts  7.04 us

profile of v3, /device:TPU:0, one launch (start us, length us, event | category | flops | bytes accessed | tf_op | source)
XLA Modules:
  0.0 82.7 jit_solution(13828595740700742336)
XLA Ops:
  2.6 73.1 %scan_backward.1 = (f32[4096,256]{1,0:T(8,128)}, bf16[128,2048]{1,0:T(8,128)(2,1)}, bf16[128,2048]{1,0:T(8,128)(2,1)}, f32[128,256]{1,0:T(8,128)}) custom-call(bf16[128,16384]{1,0:T(8,128)(2,1)} %bitcast.15, bf16[128,16384]{1,0:T(8,128)(2,1)} %bitcast.16, bf16[128,2048]{1,0:T(8,128)(2,1)} %bitcast.18, bf16[128,2048]{1,0:T(8,128)(2,1)} %bitcast.19, ...), custom_call_target="tpu_custom_call" | custom-call | flops 12884901888 | bytes 16777216 | tf_op jit(solution)/shard_map/scan_backward/pallas_call | solution.py:379
  75.6 0.0 copy-start.1
  75.7 0.0 copy-start
  75.7 0.0 copy-start.2
  75.7 4.8 %copy.22 = f32[64,64,256]{2,1,0:T(8,128)} copy(f32[64,64,256]{2,1,0:T(8,128)} %bitcast.11) | data formatting | bytes 8388608
  80.5 0.0 copy-done.1
  80.5 0.8 copy.23
  81.3 0.0 copy-done
  81.3 0.8 copy.24
  82.1 0.0 copy-done.2
  82.1 0.7 copy.25
Async XLA Ops:
  75.6 4.8 %copy-start.1 = (bf16[128,2048]{1,0:T(8,128)(2,1)S(1)}, bf16[128,2048]{1,0:T(8,128)(2,1)}, u32[]{:S(2)}) copy-start(bf16[128,2048]{1,0:T(8,128)(2,1)} %get-tuple-element.9) | copy-start | bytes 1572868
  75.7 5.6 %copy-start = (bf16[128,2048]{1,0:T(8,128)(2,1)S(1)}, bf16[128,2048]{1,0:T(8,128)(2,1)}, u32[]{:S(2)}) copy-start(bf16[128,2048]{1,0:T(8,128)(2,1)} %get-tuple-element.10) | copy-start | bytes 1572868
  75.7 6.4 %copy-start.2 = (f32[128,256]{1,0:T(8,128)S(1)}, f32[128,256]{1,0:T(8,128)}, u32[]{:S(2)}) copy-start(f32[128,256]{1,0:T(8,128)} %get-tuple-element.11) | copy-start | bytes 393220

commit v4 on v3

--- a/solution.py
+++ b/solution.py
@@ -350,6 +350,39 @@
         write.wait()
 
 
+PIECES = 8
+
+
+def copy_kernel(state_from, gb_from, gc_from, gdt_from, state_to, gb_to, gc_to, gdt_to, sem):
+    rows = state_from.shape[0] // PIECES
+    copies = [
+        pltpu.make_async_copy(
+            state_from.at[pl.ds(i * rows, rows), :], state_to.at[pl.ds(i * rows, rows), :], sem.at[i]
+        )
+        for i in range(PIECES)
+    ]
+    small = ((gb_from, gb_to), (gc_from, gc_to), (gdt_from, gdt_to))
+    for i, (source, target) in enumerate(small):
+        copies.append(pltpu.make_async_copy(source, target, sem.at[PIECES + i]))
+    for copy in copies:
+        copy.start()
+    for copy in copies:
+        copy.wait()
+
+
+def copied(*results):
+    there = pl.BlockSpec(memory_space=pl.ANY)
+    return pl.pallas_call(
+        copy_kernel,
+        in_specs=[there] * 4,
+        out_specs=[there] * 4,
+        out_shape=[jax.ShapeDtypeStruct(result.shape, result.dtype) for result in results],
+        scratch_shapes=[pltpu.SemaphoreType.DMA((PIECES + 3,))],
+        compiler_params=pltpu.CompilerParams(vmem_limit_bytes=VMEM_BYTES),
+        name="copy_results",
+    )(*results)
+
+
 def per_device(
     count,
     inputs,
@@ -376,7 +409,7 @@
     scalar = pl.BlockSpec(memory_space=pltpu.SMEM)
     dma = pltpu.SemaphoreType.DMA
     flops = 24 * tok * tok * x.shape[1] + 12 * count * tok * width * state_dim
-    grad_state, grad_b, grad_c, grad_dt = pl.pallas_call(
+    results = pl.pallas_call(
         functools.partial(kernel, count, groups, head_dim),
         in_specs=[there, there, whole, whole, whole, whole, there, whole, scalar, scalar, scalar],
         out_specs=[there, whole, whole, whole],
@@ -428,6 +461,7 @@
         adv_scale,
         lengths,
     )
+    grad_state, grad_b, grad_c, grad_dt = copied(*results)
     return grad_state.reshape(state_codes.shape), grad_b[None], grad_c[None], grad_dt[None]
 
 

time: 82.9 us -> 240 us (2.90)
  Pallas kernels: 73.1 us -> 237 us
  local copies, waits for them, and re-layouts: 7.04 us -> 0 us
    pallas_call x0 -> x1, Pallas kernels: none -> 164 us  [copied(): pl.pallas_call(copy_kernel, in_specs=[there] * 4, out_specs=[there] * 4,...]
    unnamed x10 -> x0, local copies, waits for them, and re-layouts: 7.04 us -> none
where the time goes in v4:
time: 240 us
  Pallas kernels  237 us (99%)
  between operations  2.58 us (1%)
    pallas_call x1, Pallas kernels, copied(): pl.pallas_call(copy_kernel, in_specs=[there] * 4, out_specs=[there] * 4,...  164 us
    pallas_call x1, Pallas kernels, per_device(): pl.pallas_call(functools.partial(kernel, count, groups, head_dim), in_spe...  73.1 us

profile of v4, /device:TPU:0, one launch (start us, length us, event | category | flops | bytes accessed | tf_op | source)
XLA Modules:
  0.0 239.6 jit_solution(6158962133454924270)
XLA Ops:
  2.6 73.1 %scan_backward.1 = (f32[4096,256]{1,0:T(8,128)}, bf16[128,2048]{1,0:T(8,128)(2,1)}, bf16[128,2048]{1,0:T(8,128)(2,1)}, f32[128,256]{1,0:T(8,128)}) custom-call(bf16[128,16384]{1,0:T(8,128)(2,1)} %bitcast.11, bf16[128,16384]{1,0:T(8,128)(2,1)} %bitcast.12, bf16[128,2048]{1,0:T(8,128)(2,1)} %bitcast.15, bf16[128,2048]{1,0:T(8,128)(2,1)} %bitcast.16, ...), custom_call_target="tpu_custom_call" | custom-call | flops 12884901888 | bytes 16777216 | tf_op jit(solution)/shard_map/scan_backward/pallas_call | solution.py:412
  75.6 164.0 %copy_results.1 = (f32[4096,256]{1,0:T(8,128)}, bf16[128,2048]{1,0:T(8,128)(2,1)}, bf16[128,2048]{1,0:T(8,128)(2,1)}, f32[128,256]{1,0:T(8,128)}) custom-call(f32[4096,256]{1,0:T(8,128)} %get-tuple-element.12.state_from, bf16[128,2048]{1,0:T(8,128)(2,1)} %get-tuple-element.13.gb_from, bf16[128,2048]{1,0:T(8,128)(2,1)} %get-tuple-element.14.gc_from, ...), custom_call_target="tpu_custom_call" | custom-call | tf_op jit(solution)/shard_map/copy_results/pallas_call | solution.py:375

commit v5 on v3

--- a/solution.py
+++ b/solution.py
@@ -350,6 +350,43 @@
         write.wait()
 
 
+PIECES = 8
+
+
+def copy_kernel(*refs):
+    sources, targets, staged = refs[:4], refs[4:8], refs[8:12]
+    in_sem, out_sem = refs[12:]
+    rows = sources[0].shape[0] // PIECES
+    pieces = [(0, pl.ds(i * rows, rows)) for i in range(PIECES)]
+    pieces += [(i, pl.ds(0, sources[i].shape[0])) for i in range(1, 4)]
+    loads, stores = [], []
+    for n, (i, here) in enumerate(pieces):
+        held = staged[i].at[here, :]
+        loads.append(pltpu.make_async_copy(sources[i].at[here, :], held, in_sem.at[n]))
+        stores.append(pltpu.make_async_copy(held, targets[i].at[here, :], out_sem.at[n]))
+    for load in loads:
+        load.start()
+    for load, store in zip(loads, stores):
+        load.wait()
+        store.start()
+    for store in stores:
+        store.wait()
+
+
+def copied(*results):
+    there = pl.BlockSpec(memory_space=pl.ANY)
+    return pl.pallas_call(
+        copy_kernel,
+        in_specs=[there] * 4,
+        out_specs=[there] * 4,
+        out_shape=[jax.ShapeDtypeStruct(result.shape, result.dtype) for result in results],
+        scratch_shapes=[pltpu.VMEM(result.shape, result.dtype) for result in results]
+        + [pltpu.SemaphoreType.DMA((PIECES + 3,))] * 2,
+        compiler_params=pltpu.CompilerParams(vmem_limit_bytes=VMEM_BYTES),
+        name="copy_results",
+    )(*results)
+
+
 def per_device(
     count,
     inputs,
@@ -376,7 +413,7 @@
     scalar = pl.BlockSpec(memory_space=pltpu.SMEM)
     dma = pltpu.SemaphoreType.DMA
     flops = 24 * tok * tok * x.shape[1] + 12 * count * tok * width * state_dim
-    grad_state, grad_b, grad_c, grad_dt = pl.pallas_call(
+    results = pl.pallas_call(
         functools.partial(kernel, count, groups, head_dim),
         in_specs=[there, there, whole, whole, whole, whole, there, whole, scalar, scalar, scalar],
         out_specs=[there, whole, whole, whole],
@@ -428,6 +465,7 @@
         adv_scale,
         lengths,
     )
+    grad_state, grad_b, grad_c, grad_dt = copied(*results)
     return grad_state.reshape(state_codes.shape), grad_b[None], grad_c[None], grad_dt[None]
 
 

time: 82.9 us -> 80.6 us (0.972)
  local copies, waits for them, and re-layouts: 7.04 us -> 0 us
  Pallas kernels: 73.1 us -> 77.8 us
    unnamed x10 -> x0, local copies, waits for them, and re-layouts: 7.04 us -> none
    pallas_call x0 -> x1, Pallas kernels: none -> 4.75 us  [copied(): pl.pallas_call(copy_kernel, in_specs=[there] * 4, out_specs=[there] * 4,...]
where the time goes in v5:
time: 80.6 us; the launch traced here: 80.4 us
  Pallas kernels  77.8 us (97%)
  between operations  2.58 us (3%)
    pallas_call x1, Pallas kernels, per_device(): pl.pallas_call(functools.partial(kernel, count, groups, head_dim), in_spe...  73.1 us
    pallas_call x1, Pallas kernels, copied(): pl.pallas_call(copy_kernel, in_specs=[there] * 4, out_specs=[there] * 4,...  4.75 us

profile of v5, /device:TPU:0, one launch (start us, length us, event | category | flops | bytes accessed | tf_op | source)
XLA Modules:
  0.0 80.4 jit_solution(5202477418926526211)
XLA Ops:
  2.6 73.1 %scan_backward.1 = (f32[4096,256]{1,0:T(8,128)}, bf16[128,2048]{1,0:T(8,128)(2,1)}, bf16[128,2048]{1,0:T(8,128)(2,1)}, f32[128,256]{1,0:T(8,128)}) custom-call(bf16[128,16384]{1,0:T(8,128)(2,1)} %bitcast.11, bf16[128,16384]{1,0:T(8,128)(2,1)} %bitcast.12, bf16[128,2048]{1,0:T(8,128)(2,1)} %bitcast.15, bf16[128,2048]{1,0:T(8,128)(2,1)} %bitcast.16, ...), custom_call_target="tpu_custom_call" | custom-call | flops 12884901888 | bytes 16777216 | tf_op jit(solution)/shard_map/scan_backward/pallas_call | solution.py:416
  75.6 4.7 %copy_results.1 = (f32[4096,256]{1,0:T(8,128)}, bf16[128,2048]{1,0:T(8,128)(2,1)}, bf16[128,2048]{1,0:T(8,128)(2,1)}, f32[128,256]{1,0:T(8,128)}) custom-call(f32[4096,256]{1,0:T(8,128)} %get-tuple-element.12.refs_0_, bf16[128,2048]{1,0:T(8,128)(2,1)} %get-tuple-element.13.refs_1_, bf16[128,2048]{1,0:T(8,128)(2,1)} %get-tuple-element.14.refs_2_, ...), custom_call_target="tpu_custom_call" | custom-call | tf_op jit(solution)/shard_map/copy_results/pallas_call | solution.py:378

commit v6 on v5

--- a/solution.py
+++ b/solution.py
@@ -146,12 +146,17 @@
             device_id_type=pl.DeviceIdType.MESH,
         )
 
-    def send_d(k, s):
+    last = span - 1
+    half = tok // 2
+    steps = [(s, 0, tok) for s in range(last)] + [(last, 0, half), (last, half, half)]
+
+    def send_d(k, n):
+        s, first, rows = steps[n]
         return remote(
-            d_hbm.at[:, columns(other(k), s)],
-            got_d.at[k, :, pl.ds(s * part_width, part_width)],
-            d_send.at[k, s],
-            d_recv.at[k, s],
+            d_hbm.at[pl.ds(first, rows), columns(other(k), s)],
+            got_d.at[k, pl.ds(first, rows), pl.ds(s * part_width, part_width)],
+            d_send.at[k, n],
+            d_recv.at[k, n],
             k,
         )
 
@@ -191,9 +196,9 @@
     for k in range(1, count):
         send_w(k).start()
         send_c(k).start()
-    for s in range(1, span):
+    for n in range(1, len(steps)):
         for k in range(1, count):
-            send_d(k, s).start()
+            send_d(k, n).start()
     got_c[0] = c_ref[:, state_columns(me)]
     got_w[0] = wa_ref[heads_of(me), :]
     loads[0].wait()
@@ -253,12 +258,13 @@
     for start in range(0, width, chunk):
         codes_flip[:, start : start + chunk] = codes_ref[start : start + chunk, :].T
 
-    def back_dc(k, s):
+    def back_dc(k, n):
+        s, first, rows = steps[n]
         return remote(
-            out_dc.at[k, :, pl.ds(s * state_dim, state_dim)],
-            got_dc.at[k, :, pl.ds(s * state_dim, state_dim)],
-            dc_send.at[k, s],
-            dc_recv.at[k, s],
+            out_dc.at[k, pl.ds(first, rows), pl.ds(s * state_dim, state_dim)],
+            got_dc.at[k, pl.ds(first, rows), pl.ds(s * state_dim, state_dim)],
+            dc_send.at[k, n],
+            dc_recv.at[k, n],
             -k,
         )
 
@@ -272,41 +278,42 @@
         )
 
     writes = []
+
+    def from_state(k, s, first, rows):
+        tokens = slice(first, first + rows)
+        lanes = pl.ds(pl.multiple_of(k * 2 * tok + 2 * first, 128), 2 * rows)
+        c = got_c[k, tokens, s * state_dim : (s + 1) * state_dim]
+        c_flip = c.T
+        d_c = jnp.zeros((state_dim, 2 * rows), F32)
+        for start in range(0, part_width, chunk):
+            here = slice(s * part_width + start, s * part_width + start + chunk)
+            head = s * part + start // head_dim
+            heads = slice(head, head + chunk_heads)
+            v = got_d[k, tokens, here].T.astype(F32) * over_rows(got_w[k, heads, tokens], head_dim)
+            v = v * scale_rows[here, :rows]
+            v_parts = jnp.concatenate(split(v), axis=1)
+            parts_ref[start : start + chunk, lanes] = v_parts
+            d_c += dot(codes_flip[:, here], v_parts)
+            out_dl[k, heads, tokens] = head_sums(v * dot(codes_ref[here, :], c_flip), head_dim)
+        out_dc[k, tokens, s * state_dim : (s + 1) * state_dim] = (d_c[:, :rows] + d_c[:, rows:]).T
+        c_twice[lanes, :] = jnp.concatenate([c, c], axis=0)
+
     for s in range(span):
-
-        def one_response(k, carry, s=s):
-            @pl.when(k > 0)
-            def _():
-                if s == 0:
+        from_state(0, s, 0, tok)
+        for n in [n for n in range(len(steps)) if steps[n][0] == s]:
+
+            def one_response(k, carry, n=n, s=s):
+                if n == 0:
                     send_w(k).wait_recv()
                     send_c(k).wait_recv()
-                send_d(k, s).wait_recv()
-
-            lanes = pl.ds(pl.multiple_of(k * 2 * tok, 128), 2 * tok)
-            c = got_c[k, :, s * state_dim : (s + 1) * state_dim]
-            c_flip = c.T
-            d_c = jnp.zeros((state_dim, 2 * tok), F32)
-            for start in range(0, part_width, chunk):
-                here = slice(s * part_width + start, s * part_width + start + chunk)
-                first = s * part + start // head_dim
-                heads = slice(first, first + chunk_heads)
-                v = got_d[k, :, here].T.astype(F32) * over_rows(got_w[k, heads, :], head_dim)
-                v = v * scale_rows[here, :]
-                v_parts = jnp.concatenate(split(v), axis=1)
-                parts_ref[start : start + chunk, lanes] = v_parts
-                d_c += dot(codes_flip[:, here], v_parts)
-                out_dl[k, heads, :] = head_sums(v * dot(codes_ref[here, :], c_flip), head_dim)
-            out_dc[k, :, s * state_dim : (s + 1) * state_dim] = (d_c[:, :tok] + d_c[:, tok:]).T
-
-            @pl.when(k > 0)
-            def _():
-                back_dc(k, s).start()
-                back_dl(k, s).start()
-
-            c_twice[lanes, :] = jnp.concatenate([c, c], axis=0)
-            return carry
-
-        lax.fori_loop(0, count, one_response, 0)
+                send_d(k, n).wait_recv()
+                from_state(k, *steps[n])
+                back_dc(k, n).start()
+                if steps[n][1] + steps[n][2] == tok:
+                    back_dl(k, s).start()
+                return carry
+
+            lax.fori_loop(1, count, one_response, 0)
 
         def one_chunk(j, carry, s=s):
             rows = pl.ds(pl.multiple_of(j * chunk, chunk), chunk)
@@ -328,11 +335,18 @@
         log_ref[heads_of(owner), :] = d_l
 
     add_back(me, out_dc[0], out_dl[0])
-    for k in range(1, count):
-        for s in range(span):
-            back_dc(k, s).wait_recv()
-            back_dl(k, s).wait_recv()
-        add_back(other(k), got_dc[k], got_dl[k])
+    for n, (s, first, rows) in enumerate(steps):
+        cols = slice(s * state_dim, (s + 1) * state_dim)
+        for k in range(1, count):
+            back_dc(k, n).wait_recv()
+            begin = pl.multiple_of((first_group(other(k)) + s) * state_dim, 128)
+            states = pl.ds(begin, state_dim)
+            tokens = slice(first, first + rows)
+            total_ref[tokens, states] = total_ref[tokens, states] + got_dc[k, tokens, cols]
+            if first + rows == tok:
+                back_dl(k, s).wait_recv()
+                heads = pl.ds(pl.multiple_of(other(k) * own + s * part, 8), part)
+                log_ref[heads, :] = got_dl[k, s * part : (s + 1) * part, :]
     gc_ref[...] = total_ref[...].astype(BF16)
     col = col_ref[...]
     d_log = (log_ref[...] + (row_ref[...] - col)).T
@@ -342,9 +356,10 @@
     for k in range(1, count):
         send_w(k).wait_send()
         send_c(k).wait_send()
+        for n in range(len(steps)):
+            send_d(k, n).wait_send()
+            back_dc(k, n).wait_send()
         for s in range(span):
-            send_d(k, s).wait_send()
-            back_dc(k, s).wait_send()
             back_dl(k, s).wait_send()
     for write in writes:
         write.wait()
@@ -442,9 +457,9 @@
         ]
         + [pltpu.VMEM((all_heads, tok), F32)] * 5
         + [pltpu.VMEM(c.shape, F32), dma((4,)), dma((span,))]
-        + [dma((count, span))] * 2
+        + [dma((count, span + 1))] * 2
         + [dma((count,))] * 4
-        + [dma((count, span))] * 4,
+        + [dma((count, span + 1))] * 4,
         compiler_params=pltpu.CompilerParams(
             collective_id=0, has_side_effects=True, vmem_limit_bytes=VMEM_BYTES
         ),

time: 80.6 us -> 80.8 us (level)
  no operation moved by 1% of the time
where the time goes in v6:
time: 80.8 us; the launch traced here: 80.6 us
  Pallas kernels  78.1 us (97%)
  between operations  2.58 us (3%)
    pallas_call x1, Pallas kernels, per_device(): pl.pallas_call(functools.partial(kernel, count, groups, head_dim), in_spe...  73.3 us
    pallas_call x1, Pallas kernels, copied(): pl.pallas_call(copy_kernel, in_specs=[there] * 4, out_specs=[there] * 4,...  4.75 us

profile of v6, /device:TPU:0, one launch (start us, length us, event | category | flops | bytes accessed | tf_op | source)
XLA Modules:
  0.0 80.6 jit_solution(1938958540274049109)
XLA Ops:
  2.6 73.3 %scan_backward.1 = (f32[4096,256]{1,0:T(8,128)}, bf16[128,2048]{1,0:T(8,128)(2,1)}, bf16[128,2048]{1,0:T(8,128)(2,1)}, f32[128,256]{1,0:T(8,128)}) custom-call(bf16[128,16384]{1,0:T(8,128)(2,1)} %bitcast.11, bf16[128,16384]{1,0:T(8,128)(2,1)} %bitcast.12, bf16[128,2048]{1,0:T(8,128)(2,1)} %bitcast.15, bf16[128,2048]{1,0:T(8,128)(2,1)} %bitcast.16, ...), custom_call_target="tpu_custom_call" | custom-call | flops 12884901888 | bytes 16777216 | tf_op jit(solution)/shard_map/scan_backward/pallas_call | solution.py:431
  75.9 4.7 %copy_results.1 = (f32[4096,256]{1,0:T(8,128)}, bf16[128,2048]{1,0:T(8,128)(2,1)}, bf16[128,2048]{1,0:T(8,128)(2,1)}, f32[128,256]{1,0:T(8,128)}) custom-call(f32[4096,256]{1,0:T(8,128)} %get-tuple-element.12.refs_0_, bf16[128,2048]{1,0:T(8,128)(2,1)} %get-tuple-element.13.refs_1_, bf16[128,2048]{1,0:T(8,128)(2,1)} %get-tuple-element.14.refs_2_, ...), custom_call_target="tpu_custom_call" | custom-call | tf_op jit(solution)/shard_map/copy_results/pallas_call | solution.py:393
